TPU v7x, 32 devices: a whole 2x2x4 slice. The times are simulated.
32 devices in a mesh: rows: 16 (over z, x, core), chan: 2 (over y).
Axes of the slice: x: 2, y: 2, z: 4, core: 2. Of those that a mesh axis runs over, the one named last changes fastest.
Arguments:
- feature: bfloat16 [48, 144, 1536], P('rows', None, 'chan'), may hold values from -6 to 6
- kernel: float32 [7, 7, 1536], P(None, None, 'chan'), may hold values from -0.875 to 0.875
- ln_gain: float32 [1536], replicated, may hold values from 0.1 to 1.9
- layer_scale: float32 [1536], replicated, may hold values from 0.1 to 1.9
- w_in: bfloat16 [1536, 6144], P(None, 'chan'), may hold values from -0.15625 to 0.15625
- w_out: bfloat16 [6144, 1536], P('chan'), may hold values from -0.078125 to 0.078125
- cotangent: bfloat16 [48, 144, 1536], P('rows'), may hold values from -6 to 6
Outputs:
- grad_feature: bfloat16 [48, 144, 1536], P('rows', None, 'chan')
- grad_w_in: float32 [1536, 6144], P('rows', 'chan')
- grad_w_out: float32 [6144, 1536], P('chan', 'rows')
- grad_kernel: float32 [7, 7, 1536], P(None, None, 'chan')
All inputs are finite; a program needn't handle non-finite values.
Results may differ from a plain program's by a relative error of at most 0.03.
Values may be sent and summed in bfloat16 or wider, within the bound.
A program may use at most 128 MiB of HBM per device.

v0:
```python
import math

import jax
import jax.numpy as jnp
from jax import lax
from jax.sharding import PartitionSpec as P


def halo(cells, width):
    count = lax.axis_size("rows")
    ends = count - 1
    head = cells[:width]
    tail = cells[cells.shape[0] - width :]
    above = lax.ppermute(tail, "rows", [(i, i + 1) for i in range(ends)])
    below = lax.ppermute(head, "rows", [(i + 1, i) for i in range(ends)])
    return above, below


def conv_taps(padded, kernel, height, width):
    result = jnp.zeros((height, width, kernel.shape[2]), jnp.float32)
    for tap_row in range(7):
        for tap_col in range(7):
            window = padded[tap_row : tap_row + height, tap_col : tap_col + width].astype(
                jnp.float32
            )
            result = result + window * kernel[tap_row, tap_col]
    return result


def conv_back(grad_pad, kernel, height, width):
    result = jnp.zeros((height, width, kernel.shape[2]), jnp.float32)
    for tap_row in range(7):
        for tap_col in range(7):
            window = grad_pad[
                6 - tap_row : 6 - tap_row + height, 6 - tap_col : 6 - tap_col + width
            ].astype(jnp.float32)
            result = result + window * kernel[tap_row, tap_col]
    return result


def kernel_terms(grad_conv, padded, height, width, tap_rows):
    grad_float = grad_conv.astype(jnp.float32)
    rows_list = []
    for tap_row in tap_rows:
        cols_list = []
        for tap_col in range(7):
            window = padded[tap_row : tap_row + height, tap_col : tap_col + width].astype(
                jnp.float32
            )
            cols_list.append(jnp.sum(grad_float * window, axis=(0, 1)))
        rows_list.append(jnp.stack(cols_list))
    return jnp.stack(rows_list)


def gelu_tanh(value):
    return jax.nn.gelu(value, approximate=True)


def chip_at(place, chips):
    place = lax.rem(place, chips)
    half = chips // 2
    return jnp.where(place < half, 2 * place, 2 * (chips - 1 - place) + 1)


def ring_pairs(chips, step):
    def chip(place):
        place = place % chips
        half = chips // 2
        return 2 * place if place < half else 2 * (chips - 1 - place) + 1

    return [
        (2 * chip(p) + core, 2 * chip(p + step) + core) for p in range(chips) for core in range(2)
    ]


def tie(value, *first):
    return lax.optimization_barrier((value, first))[0]


def ring_piece(part, position, side, chips):
    share = part.shape[0] // chips
    half = share // 2
    return lax.dynamic_slice_in_dim(
        part, chip_at(position, chips) * share + side * half, half, 0
    )


def ring_first(part, place, chips):
    return [ring_piece(part, place + chips - 1, 0, chips), ring_piece(part, place + 1, 1, chips)]


def ring_step(part, sums, step, place, chips):
    result = []
    for side, way in ((0, 1), (1, -1)):
        got = lax.ppermute(sums[side], "rows", ring_pairs(chips, way))
        own = ring_piece(part, place + 2 * chips - way * (2 + step), side, chips)
        total = got.astype(jnp.float32) + own.astype(jnp.float32)
        result.append(total.astype(jnp.bfloat16))
    return result


def own_rows(sums, core, swap):
    mine = jnp.where(core == 0, sums[0], sums[1])
    theirs = jnp.where(core == 0, sums[1], sums[0])
    got = lax.ppermute(theirs, "rows", swap)
    first = jnp.where(core == 0, mine, got)
    second = jnp.where(core == 0, got, mine)
    return jnp.concatenate([first, second], axis=1).astype(jnp.float32)


def shards(feature, kernel, ln_gain, layer_scale, w_in, w_out, cotangent):
    height, width, local_ch = feature.shape
    channels = cotangent.shape[2]
    pixels = height * width
    rows = lax.axis_size("rows")
    chan = lax.axis_size("chan")
    chips = rows // 2
    me = lax.axis_index("rows")
    lane = lax.axis_index("chan")
    core = lax.rem(me, 2)
    chip = lax.div(me, 2)
    level = lax.div(chip, 2)
    place = jnp.where(lax.rem(chip, 2) == 0, level, chips - 1 - level)
    swap = [(i, i ^ 1) for i in range(rows)]
    cross = [(0, 1), (1, 0)]
    scale = 1.0 / math.sqrt(height * rows * width)
    offset = lane * local_ch
    units = w_in.shape[1] // 2

    above, below = halo(feature, 3)
    grad_mixed = (cotangent.reshape(pixels, channels).astype(jnp.float32) * layer_scale).astype(
        jnp.bfloat16
    )
    mixed_both = jnp.concatenate([grad_mixed, lax.ppermute(grad_mixed, "rows", swap)], axis=0)
    in_part = lax.dynamic_slice_in_dim(w_in, core * units, units, 1)
    out_part = lax.dynamic_slice_in_dim(w_out, core * units, units, 0)
    grad_activ = lax.dot_general(
        mixed_both, out_part, (((1,), (1,)), ((), ())), preferred_element_type=jnp.float32
    )
    rimmed = jnp.concatenate([above, feature, below], axis=0)
    padded = jnp.pad(rimmed, ((0, 0), (3, 3), (0, 0)))
    conv_local = conv_taps(padded, kernel, height, width).astype(jnp.bfloat16)
    conv_local = conv_local.reshape(pixels, local_ch)
    if chan == 2:
        conv_other = lax.ppermute(conv_local, "chan", cross)
        conv_other = tie(conv_other, grad_activ)
        conv_full = jnp.concatenate(
            [
                jnp.where(lane == 0, conv_local, conv_other),
                jnp.where(lane == 0, conv_other, conv_local),
            ],
            axis=1,
        )
    else:
        conv_full = lax.all_gather(conv_local, "chan", axis=1, tiled=True)
    values = conv_full.astype(jnp.float32)
    mean = jnp.mean(values, axis=1, keepdims=True)
    centred = values - mean
    var = jnp.mean(centred * centred, axis=1, keepdims=True)
    rstd = 1.0 / jnp.sqrt(var + 1e-06)
    nhat = centred * rstd
    normed = (nhat * ln_gain).astype(jnp.bfloat16)
    normed_both = jnp.concatenate([normed, lax.ppermute(normed, "rows", swap)], axis=0)
    hidden = jnp.dot(normed_both, in_part, preferred_element_type=jnp.float32)
    activ = gelu_tanh(hidden).astype(jnp.bfloat16)
    grad_hidden = jax.vjp(gelu_tanh, hidden)[1](grad_activ)[0].astype(jnp.bfloat16)

    def pixel_sum(left, right):
        total = lax.dot_general(
            left, right, (((0,), (0,)), ((), ())), preferred_element_type=jnp.float32
        )
        return (total * scale).astype(jnp.bfloat16)

    def back(grads):
        return lax.dot_general(
            grads, in_part, (((1,), (1,)), ((), ())), preferred_element_type=jnp.float32
        )

    out_total = pixel_sum(mixed_both, activ)
    back_other = lax.ppermute(back(grad_hidden[pixels:]).astype(jnp.bfloat16), "rows", swap)
    in_total = pixel_sum(normed_both, grad_hidden)
    back_own = back(tie(grad_hidden[:pixels], in_total)) + back_other.astype(jnp.float32)

    scaled_part = back_own * ln_gain
    first_part = jnp.sum(scaled_part, axis=1)
    second_part = jnp.sum(scaled_part * nhat, axis=1)
    pair = jnp.stack([first_part, second_part])
    if chan == 2:
        kept = lax.dynamic_slice_in_dim(back_own, offset, local_ch, 1)
        given = lax.dynamic_slice_in_dim(back_own, local_ch - offset, local_ch, 1)
        sent = (given.astype(jnp.bfloat16), pair)
        got = lax.ppermute(sent[0], "chan", cross).astype(jnp.float32)
        grad_normed = kept + got
        pair = pair + lax.ppermute(pair, "chan", cross)
    else:
        sent = (back_own, pair)
        grad_normed = lax.psum_scatter(
            back_own.astype(jnp.bfloat16), "chan", scatter_dimension=1, tiled=True
        ).astype(jnp.float32)
        pair = lax.psum(pair, "chan")
    first_mean = pair[0][:, None] / channels
    second_mean = pair[1][:, None] / channels
    nhat_own = (conv_local.astype(jnp.float32) - mean) * rstd
    scaled = grad_normed * lax.dynamic_slice_in_dim(ln_gain, offset, local_ch, 0)
    grad_local = rstd * (scaled - first_mean - nhat_own * second_mean)
    grad_conv = grad_local.astype(jnp.bfloat16).reshape(height, width, local_ch)
    grad_above, grad_below = halo(grad_conv, 3)
    grad_rimmed = jnp.concatenate([grad_above, grad_conv, grad_below], axis=0)
    grad_pad = jnp.pad(grad_rimmed, ((0, 0), (3, 3), (0, 0)))
    cot_own = lax.dynamic_slice_in_dim(cotangent, offset, local_ch, 2).astype(jnp.float32)

    def terms(grads, tap_rows):
        return (kernel_terms(grads, padded, height, width, tap_rows) * scale).astype(
            jnp.bfloat16
        )

    kernel_sum = None
    grad_feature = None
    span = 1
    totals = [out_total, in_total]
    sums = [ring_first(total, place, chips) for total in totals]
    last = chips - 2
    for step in range(chips - 1):
        for which in range(2):
            if step == 1 and which == 1:
                sums[which] = tie(sums[which], sent)
            if step == 3 and which == 0:
                sums[which] = tie(sums[which], grad_conv)
            if step == 4 and which == 0:
                kernel_sum = terms(tie(grad_conv, early), range(7))
                sums[which] = tie(sums[which], kernel_sum)
            if step == last and which == 1:
                grad_feature = (
                    cot_own + conv_back(tie(grad_pad, middle), kernel, height, width)
                ).astype(jnp.bfloat16)
                sums[which] = tie(sums[which], grad_feature)
            if step > 4 and span < rows:
                other = lax.ppermute(kernel_sum, "rows", [(i, i ^ span) for i in range(rows)])
                total = kernel_sum.astype(jnp.float32) + other.astype(jnp.float32)
                span *= 2
                kernel_sum = total if span >= rows else total.astype(jnp.bfloat16)
                sums[which] = tie(sums[which], kernel_sum)
            sums[which] = ring_step(totals[which], sums[which], step, place, chips)
        if step == 1:
            early = list(sums)
        if step == 3:
            middle = list(sums)
    while span < rows:
        other = lax.ppermute(kernel_sum, "rows", [(i, i ^ span) for i in range(rows)])
        total = kernel_sum.astype(jnp.float32) + other.astype(jnp.float32)
        span *= 2
        kernel_sum = total if span >= rows else total.astype(jnp.bfloat16)
    grad_w_out = own_rows(sums[0], core, swap).T
    grad_w_in = own_rows(sums[1], core, swap)
    return (grad_feature, grad_w_in, grad_w_out, kernel_sum)


def solution(mesh):
    placed = (
        P("rows", None, "chan"),
        P(None, None, "chan"),
        P(),
        P(),
        P(None, "chan"),
        P("chan", None),
        P("rows", None, None),
    )
    return jax.shard_map(
        shards,
        mesh=mesh,
        in_specs=placed,
        out_specs=(
            P("rows", None, "chan"),
            P("rows", "chan"),
            P("chan", "rows"),
            P(None, None, "chan"),
        ),
        check_vma=False,
    )
```

profile of v0, /device:TPU:0, one launch (start us, length us, event | category | flops | bytes accessed | tf_op | source)
XLA Modules:
  0.0 217.5 jit_solution(4214287793891058963)
XLA Ops:
  0.6 1.4 collective-permute-start.1
  2.1 3.1 %collective-permute-start = (bf16[3,144,768]{2,1,0:T(8,128)(2,1)}, bf16[3,144,768]{2,1,0:T(8,128)(2,1)S(1)}, u32[]{:S(2)}, u32[]{:S(2)}) collective-permute-start(bf16[3,144,768]{2,1,0:T(8,128)(2,1)} %param.7), channel_id=1, source_target_pairs={{0,2},{2,4},{4,6},{6,8},{8,10},{10,12},{12,14},{14,16},{16,18},{18... | collective-permute-start | bytes 1990664 | tf_op jit(solution)/shard_map/ppermute | solution.py:14
  5.2 2.7 %fusion.28 = bf16[432,1536]{1,0:T(8,128)(2,1)} fusion(bf16[3,144,1536]{2,1,0:T(8,128)(2,1)} %param.13, f32[1536]{0:T(1024)} %param.10), kind=kLoop, calls=%fused_computation.87 | loop fusion | flops 1990656 | bytes 2660352 | tf_op jit(solution)/shard_map/convert_element_type | solution.py:131
  7.8 2.5 %collective-permute-start.3 = (bf16[432,1536]{1,0:T(8,128)(2,1)}, bf16[432,1536]{1,0:T(8,128)(2,1)}, u32[]{:S(2)}, u32[]{:S(2)}) collective-permute-start(bf16[432,1536]{1,0:T(8,128)(2,1)} %fusion.28), channel_id=1, source_target_pairs={{0,2},{2,0},{4,6},{6,4},{8,10},{10,8},{12,14},{14,12},{16,18},{18,... | collective-permute-start | bytes 3981320 | tf_op jit(solution)/shard_map/ppermute | solution.py:134
  11.8 2.0 fusion.37
  15.1 9.8 %fusion.136 = bf16[3,144,768]{2,1,0:T(8,128)(2,1)S(1)} fusion(bf16[3,144,768]{2,1,0:T(8,128)(2,1)S(1)} %collective-permute-done.1, bf16[3,144,768]{2,1,0:T(8,128)(2,1)S(1)} %copy-done, bf16[3,144,768]{2,1,0:T(8,128)(2,1)S(1)} %copy-done.5, f32[768]{0:T(1024)S(1)} %get-tuple-element.146, f32[768]{0:T(1024)S(1)} %get-tuple-element.147, ...), kind=kLoop, calls=%fused_computation.252 | loop fusion | flops 48771072 | bytes 33328128 | tf_op jit(solution)/shard_map/convert_element_type | solution.py:142
  24.9 1.6 collective-permute-start.2
  26.5 7.9 %fusion.9 = f32[864,1536]{1,0:T(8,128)} fusion(bf16[3072,1536]{1,0:T(8,128)(2,1)S(1)} %bitcast.44, s32[]{:T(128)S(6)} %select_n.194, bf16[432,1536]{1,0:T(8,128)(2,1)} %collective-permute-done.3, bf16[432,1536]{1,0:T(8,128)(2,1)} %fusion.28), kind=kOutput, calls=%fused_computation.65 | convolution fusion | flops 4082171904 | bytes 12681220 | tf_op jit(solution)/shard_map/dot_general | solution.py:137
  36.6 1.6 fusion.25
  38.3 9.6 %collective-permute-start.4 = (bf16[432,1536]{1,0:T(8,128)(2,1)}, bf16[432,1536]{1,0:T(8,128)(2,1)}, u32[]{:S(2)}, u32[]{:S(2)}) collective-permute-start(bf16[432,1536]{1,0:T(8,128)(2,1)} %fusion.25), channel_id=1, source_target_pairs={{0,2},{2,0},{4,6},{6,4},{8,10},{10,8},{12,14},{14,12},{16,18},{18,... | collective-permute-start | bytes 3981320 | tf_op jit(solution)/shard_map/ppermute | solution.py:163
  49.2 1.7 collective-permute-done.4
  50.9 10.2 %fusion.8 = (bf16[864,1536]{1,0:T(8,128)(2,1)S(1)}, f32[864,1536]{1,0:T(8,128)S(1)}) fusion(f32[864,1536]{1,0:T(8,128)} %fusion.9, bf16[1536,3072]{1,0:T(8,128)(2,1)} %param.11, s32[]{:T(128)S(6)} %select_n.194, bf16[432,1536]{1,0:T(8,128)(2,1)} %collective-permute-done.4, bf16[432,1536]{1,0:T(8,128)(2,1)} %fusion.25), kind=kOutput, calls=%fused_computation.63 | convolution fusion | flops 4108713984 | bytes 20643844 | tf_op jit(solution)/shard_map/dot_general | solution.py:164
  61.1 7.4 %fusion.1 = bf16[1536,1536]{1,0:T(8,128)(2,1)S(1)} fusion(f32[864,1536]{1,0:T(8,128)S(1)} %get-tuple-element.193, bf16[432,1536]{1,0:T(8,128)(2,1)} %collective-permute-done.3, bf16[432,1536]{1,0:T(8,128)(2,1)} %fusion.28), kind=kOutput, calls=%fused_computation.54 | convolution fusion | flops 4098834432 | bytes 12681216 | tf_op jit(solution)/shard_map/dot_general | solution.py:169
  68.6 4.2 %collective-permute-start.13 = (bf16[96,1536]{1,0:T(8,128)(2,1)S(1)}, bf16[96,1536]{1,0:T(8,128)(2,1)S(1)}, u32[]{:S(2)}, u32[]{:S(2)}) collective-permute-start(bf16[96,1536]{1,0:T(8,128)(2,1)S(1)} %get-tuple-element.180), channel_id=1, source_target_pairs={{0,4},{2,6},{8,0},{10,2},{16,8},{18,10},{24,16},{26,18},{28,24},{3... | collective-permute-start | bytes 884744 | tf_op jit(solution)/shard_map/ppermute | solution.py:95
  72.8 2.3 %collective-permute-start.10 = (bf16[96,1536]{1,0:T(8,128)(2,1)S(1)}, bf16[96,1536]{1,0:T(8,128)(2,1)S(1)}, u32[]{:S(2)}, u32[]{:S(2)}) collective-permute-start(bf16[96,1536]{1,0:T(8,128)(2,1)S(1)} %get-tuple-element.181), channel_id=1, source_target_pairs={{0,8},{2,10},{8,16},{10,18},{16,24},{18,26},{24,28},{26,30},{28,20... | collective-permute-start | bytes 884744 | tf_op jit(solution)/shard_map/ppermute | solution.py:95
  75.2 7.3 %fusion = bf16[1536,1536]{1,0:T(8,128)(2,1)S(1)} fusion(bf16[864,1536]{1,0:T(8,128)(2,1)S(1)} %get-tuple-element.192, bf16[432,1536]{1,0:T(8,128)(2,1)} %collective-permute-done.4, bf16[432,1536]{1,0:T(8,128)(2,1)} %fusion.25), kind=kOutput, calls=%fused_computation.53 | convolution fusion | flops 4086890496 | bytes 10027008 | tf_op jit(solution)/shard_map/dot_general | solution.py:169
  82.6 2.0 collective-permute-start.18
  84.6 2.3 %fusion.22 = bf16[432,1536]{1,0:T(8,128)(2,1)S(1)} fusion(bf16[1536,3072]{1,0:T(8,128)(2,1)S(1)} %bitcast.46, s32[]{:T(128)S(6)} %select_n.194, bf16[864,1536]{1,0:T(8,128)(2,1)S(1)} %get-tuple-element.192), kind=kOutput, calls=%fused_computation.80 | convolution fusion | flops 2039095296 | bytes 7372804 | tf_op jit(solution)/shard_map/dot_general | solution.py:175
  87.3 2.0 collective-permute-start.11
  89.2 3.2 %collective-permute-done.19 = bf16[96,1536]{1,0:T(8,128)(2,1)S(1)} collective-permute-done((bf16[96,1536]{1,0:T(8,128)(2,1)S(1)}, bf16[96,1536]{1,0:T(8,128)(2,1)S(1)}, u32[]{:S(2)}, u32[]{:S(2)}) %collective-permute-start.19) | collective-permute-done | bytes 294944 | tf_op jit(solution)/shard_map/ppermute | solution.py:95
  92.7 5.2 %collective-permute-done.14 = bf16[96,1536]{1,0:T(8,128)(2,1)S(1)} collective-permute-done((bf16[96,1536]{1,0:T(8,128)(2,1)S(1)}, bf16[96,1536]{1,0:T(8,128)(2,1)S(1)}, u32[]{:S(2)}, u32[]{:S(2)}) %collective-permute-start.14) | collective-permute-done | bytes 294944 | tf_op jit(solution)/shard_map/ppermute | solution.py:95
  99.4 1.5 collective-permute-start.12
  101.0 2.8 %multiply_reduce_fusion = (f32[432]{0:T(512)S(1)}, f32[432]{0:T(512)S(1)}, f32[432,1536]{1,0:T(8,128)S(1)}) fusion(f32[1536]{0:T(1024)S(1)} %copy-done.56, f32[432]{0:T(512)S(1)} %copy-done.58, f32[432]{0:T(512)S(1)} %copy-done.54, bf16[432,768]{1,0:T(8,128)(2,1)S(1)} %get-tuple-element.183, bf16[432,768]{1,0:T(8,128)(2,1)S(1)} %get-tuple-element.182, ...), kind=kOutput, calls=%fused_computation.93 | convolution fusion | flops 2046393600 | bytes 11369860 | tf_op jit(solution)/shard_map/dot_general | solution.py:175
  103.8 1.6 collective-permute-start.7
  106.1 1.7 collective-permute-start.20
  108.6 6.1 %collective-permute-done.20 = bf16[96,1536]{1,0:T(8,128)(2,1)S(1)} collective-permute-done((bf16[96,1536]{1,0:T(8,128)(2,1)S(1)}, bf16[96,1536]{1,0:T(8,128)(2,1)S(1)}, u32[]{:S(2)}, u32[]{:S(2)}) %collective-permute-start.20) | collective-permute-done | bytes 294944 | tf_op jit(solution)/shard_map/ppermute | solution.py:95
  115.5 1.7 collective-permute-start.24
  117.5 3.3 %collective-permute-done.6 = bf16[432,768]{1,0:T(8,128)(2,1)S(1)} collective-permute-done((bf16[432,768]{1,0:T(8,128)(2,1)S(1)}, bf16[432,768]{1,0:T(8,128)(2,1)S(1)}, u32[]{:S(2)}, u32[]{:S(2)}) %collective-permute-start.6) | collective-permute-done | bytes 663584 | tf_op jit(solution)/shard_map/ppermute | solution.py:192
  121.4 3.2 %fusion.133 = (f32[768]{0:T(1024)S(1)}, f32[768]{0:T(1024)S(1)}, f32[768]{0:T(1024)S(1)}, f32[768]{0:T(1024)S(1)}, f32[768]{0:T(1024)S(1)}, /*index=5*/f32[768]{...) fusion(bf16[3,144,768]{2,1,0:T(8,128)(2,1)S(1)} %bitcast.30, ...), kind=kLoop, calls=%fused_computation.245 | loop fusion | flops 18233856 | bytes 12662784 | tf_op jit(solution)/shard_map/reduce_sum | solution.py:50
  124.7 3.3 %fusion.134 = (f32[768]{0:T(1024)S(1)}, f32[768]{0:T(1024)S(1)}, f32[768]{0:T(1024)S(1)}, f32[768]{0:T(1024)S(1)}, f32[768]{0:T(1024)S(1)}, /*index=5*/f32[768]{...) fusion(bf16[3,144,768]{2,1,0:T(8,128)(2,1)S(1)} %bitcast.31, ...), kind=kLoop, calls=%fused_computation.246 | loop fusion | flops 18233856 | bytes 12662784 | tf_op jit(solution)/shard_map/reduce_sum | solution.py:50
  128.0 2.1 fusion.132
  136.0 1.4 add_convert_fusion.23
  138.7 3.1 %collective-permute-start.8 = (bf16[3,144,768]{2,1,0:T(8,128)(2,1)S(1)}, bf16[3,144,768]{2,1,0:T(8,128)(2,1)S(1)}, u32[]{:S(2)}, u32[]{:S(2)}) collective-permute-start(bf16[3,144,768]{2,1,0:T(8,128)(2,1)S(1)} %bitcast.34), channel_id=1, source_target_pairs={{0,2},{2,4},{4,6},{6,8},{8,10},{10,12},{12,14},{14,16},{16,18},{18... | collective-permute-start | bytes 1990664 | tf_op jit(solution)/shard_map/ppermute | solution.py:14
  141.8 8.4 %collective-permute-done.29 = bf16[7,7,768]{2,1,0:T(8,128)(2,1)S(1)} collective-permute-done((bf16[7,7,768]{2,1,0:T(8,128)(2,1)S(1)}, bf16[7,7,768]{2,1,0:T(8,128)(2,1)S(1)}, u32[]{:S(2)}, u32[]{:S(2)}) %collective-permute-start.29) | collective-permute-done | bytes 75296 | tf_op jit(solution)/shard_map/ppermute | solution.py:238
  150.2 2.5 %collective-permute-start.17 = (bf16[96,1536]{1,0:T(8,128)(2,1)S(1)}, bf16[96,1536]{1,0:T(8,128)(2,1)S(1)}, u32[]{:S(2)}, u32[]{:S(2)}) collective-permute-start(bf16[96,1536]{1,0:T(8,128)(2,1)S(1)} %get-tuple-element.27), channel_id=1, source_target_pairs={{0,4},{2,6},{8,0},{10,2},{16,8},{18,10},{24,16},{26,18},{28,24},{3... | collective-permute-start | bytes 884744 | tf_op jit(solution)/shard_map/ppermute | solution.py:95
  153.9 6.2 %collective-permute-done.32 = bf16[7,7,768]{2,1,0:T(8,128)(2,1)S(1)} collective-permute-done((bf16[7,7,768]{2,1,0:T(8,128)(2,1)S(1)}, bf16[7,7,768]{2,1,0:T(8,128)(2,1)S(1)}, u32[]{:S(2)}, u32[]{:S(2)}) %collective-permute-start.32) | collective-permute-done | bytes 75296 | tf_op jit(solution)/shard_map/ppermute | solution.py:238
  160.1 2.5 %collective-permute-start.27 = (bf16[96,1536]{1,0:T(8,128)(2,1)S(1)}, bf16[96,1536]{1,0:T(8,128)(2,1)S(1)}, u32[]{:S(2)}, u32[]{:S(2)}) collective-permute-start(bf16[96,1536]{1,0:T(8,128)(2,1)S(1)} %get-tuple-element.162), channel_id=1, source_target_pairs={{0,4},{2,6},{8,0},{10,2},{16,8},{18,10},{24,16},{26,18},{28,24},{3... | collective-permute-start | bytes 884744 | tf_op jit(solution)/shard_map/ppermute | solution.py:95
  164.1 5.9 %collective-permute-done.33 = bf16[7,7,768]{2,1,0:T(8,128)(2,1)S(1)} collective-permute-done((bf16[7,7,768]{2,1,0:T(8,128)(2,1)S(1)}, bf16[7,7,768]{2,1,0:T(8,128)(2,1)S(1)}, u32[]{:S(2)}, u32[]{:S(2)}) %collective-permute-start.33) | collective-permute-done | bytes 75296 | tf_op jit(solution)/shard_map/ppermute | solution.py:238
  169.9 3.6 %collective-permute-start.37 = (bf16[96,1536]{1,0:T(8,128)(2,1)S(1)}, bf16[96,1536]{1,0:T(8,128)(2,1)S(1)}, u32[]{:S(2)}, u32[]{:S(2)}) collective-permute-start(bf16[96,1536]{1,0:T(8,128)(2,1)S(1)} %get-tuple-element.38), channel_id=1, source_target_pairs={{0,8},{2,10},{8,16},{10,18},{16,24},{18,26},{24,28},{26,30},{28,20... | collective-permute-start | bytes 884744 | tf_op jit(solution)/shard_map/ppermute | solution.py:95
  174.2 3.6 %collective-permute-start.38 = (bf16[96,1536]{1,0:T(8,128)(2,1)S(1)}, bf16[96,1536]{1,0:T(8,128)(2,1)S(1)}, u32[]{:S(2)}, u32[]{:S(2)}) collective-permute-start(bf16[96,1536]{1,0:T(8,128)(2,1)S(1)} %get-tuple-element.39), channel_id=1, source_target_pairs={{0,4},{2,6},{8,0},{10,2},{16,8},{18,10},{24,16},{26,18},{28,24},{3... | collective-permute-start | bytes 884744 | tf_op jit(solution)/shard_map/ppermute | solution.py:95
  179.0 6.0 %collective-permute-done.37 = bf16[96,1536]{1,0:T(8,128)(2,1)S(1)} collective-permute-done((bf16[96,1536]{1,0:T(8,128)(2,1)S(1)}, bf16[96,1536]{1,0:T(8,128)(2,1)S(1)}, u32[]{:S(2)}, u32[]{:S(2)}) %collective-permute-start.37) | collective-permute-done | bytes 294944 | tf_op jit(solution)/shard_map/ppermute | solution.py:95
  185.0 2.0 collective-permute-start.31
  188.4 2.0 collective-permute-start.40
  191.4 10.7 %add_convert_fusion = bf16[3,144,768]{2,1,0:T(8,128)(2,1)} fusion(bf16[9,150,768]{2,1,0:T(8,128)(2,1)S(1)} %select_maximum_fusion, f32[768]{0:T(1024)S(1)} %get-tuple-element.146, f32[768]{0:T(1024)S(1)} %get-tuple-element.147, f32[768]{0:T(1024)S(1)} %get-tuple-element.100, f32[768]{0:T(1024)S(1)} %get-tuple-element.101, f32[768]{0:T(1024)S(1)} %get-tuple-element.102, ...), kind=kLoop, calls=%fused_computation.249 | loop fusion | flops 49434624 | bytes 33991684 | tf_op jit(solution)/shard_map/convert_element_type | solution.py:235
  203.4 2.0 collective-permute-start.35
  206.7 2.0 collective-permute-start.42
  208.6 1.4 collective-permute-done.34
  211.4 1.9 collective-permute-done.41
  (295 shorter events, 32.9 us)
Async XLA Ops:
  0.6 11.2 %collective-permute-start.1 = (bf16[3,144,768]{2,1,0:T(8,128)(2,1)}, bf16[3,144,768]{2,1,0:T(8,128)(2,1)S(1)}, u32[]{:S(2)}, u32[]{:S(2)}) collective-permute-start(bf16[3,144,768]{2,1,0:T(8,128)(2,1)} %param.7), channel_id=1, source_target_pairs={{2,0},{4,2},{6,4},{8,6},{10,8},{12,10},{14,12},{16,14},{18,16},{20... | collective-permute-start | bytes 1990664 | tf_op jit(solution)/shard_map/ppermute | solution.py:15
  2.1 8.9 %collective-permute-start = (bf16[3,144,768]{2,1,0:T(8,128)(2,1)}, bf16[3,144,768]{2,1,0:T(8,128)(2,1)S(1)}, u32[]{:S(2)}, u32[]{:S(2)}) collective-permute-start(bf16[3,144,768]{2,1,0:T(8,128)(2,1)} %param.7), channel_id=1, source_target_pairs={{0,2},{2,4},{4,6},{6,8},{8,10},{10,12},{12,14},{14,16},{16,18},{18... | collective-permute-start | bytes 1990664 | tf_op jit(solution)/shard_map/ppermute | solution.py:14
  7.8 18.7 %collective-permute-start.3 = (bf16[432,1536]{1,0:T(8,128)(2,1)}, bf16[432,1536]{1,0:T(8,128)(2,1)}, u32[]{:S(2)}, u32[]{:S(2)}) collective-permute-start(bf16[432,1536]{1,0:T(8,128)(2,1)} %fusion.28), channel_id=1, source_target_pairs={{0,2},{2,0},{4,6},{6,4},{8,10},{10,8},{12,14},{14,12},{16,18},{18,... | collective-permute-start | bytes 3981320 | tf_op jit(solution)/shard_map/ppermute | solution.py:134
  24.9 10.7 %collective-permute-start.2 = (bf16[432,768]{1,0:T(8,128)(2,1)S(1)}, bf16[432,768]{1,0:T(8,128)(2,1)S(1)}, u32[]{:S(2)}, u32[]{:S(2)}) collective-permute-start(bf16[432,768]{1,0:T(8,128)(2,1)S(1)} %bitcast.36), channel_id=1, source_target_pairs={{0,1},{1,0},{2,3},{3,2},{4,5},{5,4},{6,7},{7,6},{8,9},{9,8},{10,11... | collective-permute-start | bytes 1990664 | tf_op jit(solution)/shard_map/ppermute | solution.py:145
  38.3 12.6 %collective-permute-start.4 = (bf16[432,1536]{1,0:T(8,128)(2,1)}, bf16[432,1536]{1,0:T(8,128)(2,1)}, u32[]{:S(2)}, u32[]{:S(2)}) collective-permute-start(bf16[432,1536]{1,0:T(8,128)(2,1)} %fusion.25), channel_id=1, source_target_pairs={{0,2},{2,0},{4,6},{6,4},{8,10},{10,8},{12,14},{14,12},{16,18},{18,... | collective-permute-start | bytes 3981320 | tf_op jit(solution)/shard_map/ppermute | solution.py:163
  68.5 29.4 %copy-start.13 = (bf16[1536,1536]{1,0:T(8,128)(2,1)}, bf16[1536,1536]{1,0:T(8,128)(2,1)S(1)}, u32[]{:S(2)}) copy-start(bf16[1536,1536]{1,0:T(8,128)(2,1)S(1)} %fusion.1) | copy-start | bytes 14155780
  68.6 18.4 %collective-permute-start.13 = (bf16[96,1536]{1,0:T(8,128)(2,1)S(1)}, bf16[96,1536]{1,0:T(8,128)(2,1)S(1)}, u32[]{:S(2)}, u32[]{:S(2)}) collective-permute-start(bf16[96,1536]{1,0:T(8,128)(2,1)S(1)} %get-tuple-element.180), channel_id=1, source_target_pairs={{0,4},{2,6},{8,0},{10,2},{16,8},{18,10},{24,16},{26,18},{28,24},{3... | collective-permute-start | bytes 884744 | tf_op jit(solution)/shard_map/ppermute | solution.py:95
  72.8 14.2 %collective-permute-start.10 = (bf16[96,1536]{1,0:T(8,128)(2,1)S(1)}, bf16[96,1536]{1,0:T(8,128)(2,1)S(1)}, u32[]{:S(2)}, u32[]{:S(2)}) collective-permute-start(bf16[96,1536]{1,0:T(8,128)(2,1)S(1)} %get-tuple-element.181), channel_id=1, source_target_pairs={{0,8},{2,10},{8,16},{10,18},{16,24},{18,26},{24,28},{26,30},{28,20... | collective-permute-start | bytes 884744 | tf_op jit(solution)/shard_map/ppermute | solution.py:95
  82.5 32.2 %copy-start.14 = (bf16[1536,1536]{1,0:T(8,128)(2,1)}, bf16[1536,1536]{1,0:T(8,128)(2,1)S(1)}, u32[]{:S(2)}) copy-start(bf16[1536,1536]{1,0:T(8,128)(2,1)S(1)} %fusion) | copy-start | bytes 14155780
  82.5 9.9 %collective-permute-start.19 = (bf16[96,1536]{1,0:T(8,128)(2,1)S(1)}, bf16[96,1536]{1,0:T(8,128)(2,1)S(1)}, u32[]{:S(2)}, u32[]{:S(2)}) collective-permute-start(bf16[96,1536]{1,0:T(8,128)(2,1)S(1)} %get-tuple-element.170), channel_id=1, source_target_pairs={{0,4},{2,6},{8,0},{10,2},{16,8},{18,10},{24,16},{26,18},{28,24},{3... | collective-permute-start | bytes 884744 | tf_op jit(solution)/shard_map/ppermute | solution.py:95
  82.6 9.9 %collective-permute-start.18 = (bf16[96,1536]{1,0:T(8,128)(2,1)S(1)}, bf16[96,1536]{1,0:T(8,128)(2,1)S(1)}, u32[]{:S(2)}, u32[]{:S(2)}) collective-permute-start(bf16[96,1536]{1,0:T(8,128)(2,1)S(1)} %get-tuple-element.171), channel_id=1, source_target_pairs={{0,8},{2,10},{8,16},{10,18},{16,24},{18,26},{24,28},{26,30},{28,20... | collective-permute-start | bytes 884744 | tf_op jit(solution)/shard_map/ppermute | solution.py:95
  86.9 14.1 %collective-permute-start.5 = (bf16[432,1536]{1,0:T(8,128)(2,1)S(1)}, bf16[432,1536]{1,0:T(8,128)(2,1)S(1)}, u32[]{:S(2)}, u32[]{:S(2)}) collective-permute-start(bf16[432,1536]{1,0:T(8,128)(2,1)S(1)} %fusion.22), channel_id=1, source_target_pairs={{0,2},{2,0},{4,6},{6,4},{8,10},{10,8},{12,14},{14,12},{16,18},{18,... | collective-permute-start | bytes 3981320 | tf_op jit(solution)/shard_map/ppermute | solution.py:180
  87.1 10.8 %collective-permute-start.14 = (bf16[96,1536]{1,0:T(8,128)(2,1)S(1)}, bf16[96,1536]{1,0:T(8,128)(2,1)S(1)}, u32[]{:S(2)}, u32[]{:S(2)}) collective-permute-start(bf16[96,1536]{1,0:T(8,128)(2,1)S(1)} %get-tuple-element.178), channel_id=1, source_target_pairs={{0,4},{2,6},{8,0},{10,2},{16,8},{18,10},{24,16},{26,18},{28,24},{3... | collective-permute-start | bytes 884744 | tf_op jit(solution)/shard_map/ppermute | solution.py:95
  87.3 10.7 %collective-permute-start.11 = (bf16[96,1536]{1,0:T(8,128)(2,1)S(1)}, bf16[96,1536]{1,0:T(8,128)(2,1)S(1)}, u32[]{:S(2)}, u32[]{:S(2)}) collective-permute-start(bf16[96,1536]{1,0:T(8,128)(2,1)S(1)} %get-tuple-element.179), channel_id=1, source_target_pairs={{0,8},{2,10},{8,16},{10,18},{16,24},{18,26},{24,28},{26,30},{28,20... | collective-permute-start | bytes 884744 | tf_op jit(solution)/shard_map/ppermute | solution.py:95
  98.9 37.1 %collective-permute-start.15 = (bf16[96,1536]{1,0:T(8,128)(2,1)}, bf16[96,1536]{1,0:T(8,128)(2,1)}, u32[]{:S(2)}, u32[]{:S(2)}) collective-permute-start(bf16[96,1536]{1,0:T(8,128)(2,1)} %get-tuple-element.176), channel_id=1, source_target_pairs={{0,4},{2,6},{8,0},{10,2},{16,8},{18,10},{24,16},{26,18},{28,24},{3... | collective-permute-start | bytes 884744 | tf_op jit(solution)/shard_map/ppermute | solution.py:95
  99.4 36.6 %collective-permute-start.12 = (bf16[96,1536]{1,0:T(8,128)(2,1)}, bf16[96,1536]{1,0:T(8,128)(2,1)}, u32[]{:S(2)}, u32[]{:S(2)}) collective-permute-start(bf16[96,1536]{1,0:T(8,128)(2,1)} %get-tuple-element.177), channel_id=1, source_target_pairs={{0,8},{2,10},{8,16},{10,18},{16,24},{18,26},{24,28},{26,30},{28,20... | collective-permute-start | bytes 884744 | tf_op jit(solution)/shard_map/ppermute | solution.py:95
  103.8 3.9 %collective-permute-start.7 = (f32[2,432]{1,0:T(2,128)S(1)}, f32[2,432]{1,0:T(2,128)S(1)}, u32[]{:S(2)}, u32[]{:S(2)}) collective-permute-start(f32[2,432]{1,0:T(2,128)S(1)} %pad_maximum_fusion.7), channel_id=1, source_target_pairs={{0,1},{1,0},{2,3},{3,2},{4,5},{5,4},{6,7},{7,6},{8,9},{9,8},{10,11... | collective-permute-start | bytes 10376 | tf_op jit(solution)/shard_map/ppermute | solution.py:194
  105.4 15.4 %copy-start.12 = (bf16[3,144,768]{2,1,0:T(8,128)(2,1)S(1)}, bf16[3,144,768]{2,1,0:T(8,128)(2,1)}, u32[]{:S(2)}) copy-start(bf16[3,144,768]{2,1,0:T(8,128)(2,1)} %copy-done.11) | copy-start | bytes 1990660
  105.4 15.4 %copy-start.59 = (f32[768]{0:T(1024)S(1)}, f32[768]{0:T(1024)}, u32[]{:S(2)}) copy-start(f32[768]{0:T(1024)} %dynamic_slice.119) | copy-start | bytes 9220
  105.5 15.3 %collective-permute-start.6 = (bf16[432,768]{1,0:T(8,128)(2,1)S(1)}, bf16[432,768]{1,0:T(8,128)(2,1)S(1)}, u32[]{:S(2)}, u32[]{:S(2)}) collective-permute-start(bf16[432,768]{1,0:T(8,128)(2,1)S(1)} %dynamic-slice_convert_fusion), channel_id=1, source_target_pairs={{0,1},{1,0},{2,3},{3,2},{4,5},{5,4},{6,7},{7,6},{8,9},{9,8},{10,11... | collective-permute-start | bytes 1990664 | tf_op jit(solution)/shard_map/ppermute | solution.py:192
  106.1 8.5 %collective-permute-start.20 = (bf16[96,1536]{1,0:T(8,128)(2,1)S(1)}, bf16[96,1536]{1,0:T(8,128)(2,1)S(1)}, u32[]{:S(2)}, u32[]{:S(2)}) collective-permute-start(bf16[96,1536]{1,0:T(8,128)(2,1)S(1)} %get-tuple-element.28), channel_id=1, source_target_pairs={{0,8},{2,10},{8,16},{10,18},{16,24},{18,26},{24,28},{26,30},{28,20... | collective-permute-start | bytes 884744 | tf_op jit(solution)/shard_map/ppermute | solution.py:95
  107.8 6.8 %collective-permute-start.23 = (bf16[96,1536]{1,0:T(8,128)(2,1)S(1)}, bf16[96,1536]{1,0:T(8,128)(2,1)S(1)}, u32[]{:S(2)}, u32[]{:S(2)}) collective-permute-start(bf16[96,1536]{1,0:T(8,128)(2,1)S(1)} %get-tuple-element.29), channel_id=1, source_target_pairs={{0,4},{2,6},{8,0},{10,2},{16,8},{18,10},{24,16},{26,18},{28,24},{3... | collective-permute-start | bytes 884744 | tf_op jit(solution)/shard_map/ppermute | solution.py:95
  115.5 15.7 %collective-permute-start.24 = (bf16[96,1536]{1,0:T(8,128)(2,1)}, bf16[96,1536]{1,0:T(8,128)(2,1)S(1)}, u32[]{:S(2)}, u32[]{:S(2)}) collective-permute-start(bf16[96,1536]{1,0:T(8,128)(2,1)} %get-tuple-element.166), channel_id=1, source_target_pairs={{0,4},{2,6},{8,0},{10,2},{16,8},{18,10},{24,16},{26,18},{28,24},{3... | collective-permute-start | bytes 884744 | tf_op jit(solution)/shard_map/ppermute | solution.py:95
  117.2 14.0 %collective-permute-start.21 = (bf16[96,1536]{1,0:T(8,128)(2,1)S(1)}, bf16[96,1536]{1,0:T(8,128)(2,1)}, u32[]{:S(2)}, u32[]{:S(2)}) collective-permute-start(bf16[96,1536]{1,0:T(8,128)(2,1)S(1)} %get-tuple-element.167), channel_id=1, source_target_pairs={{0,8},{2,10},{8,16},{10,18},{16,24},{18,26},{24,28},{26,30},{28,20... | collective-permute-start | bytes 884744 | tf_op jit(solution)/shard_map/ppermute | solution.py:95
  131.1 3.5 %collective-permute-start.28 = (bf16[7,7,768]{2,1,0:T(8,128)(2,1)S(1)}, bf16[7,7,768]{2,1,0:T(8,128)(2,1)S(1)}, u32[]{:S(2)}, u32[]{:S(2)}) collective-permute-start(bf16[7,7,768]{2,1,0:T(8,128)(2,1)S(1)} %multiply_convert_fusion.3), channel_id=1, source_target_pairs={{0,2},{2,0},{4,6},{6,4},{8,10},{10,8},{12,14},{14,12},{16,18},{18,... | collective-permute-start | bytes 225800 | tf_op jit(solution)/shard_map/ppermute | solution.py:238
  132.6 17.6 %collective-permute-start.25 = (bf16[96,1536]{1,0:T(8,128)(2,1)S(1)}, bf16[96,1536]{1,0:T(8,128)(2,1)S(1)}, u32[]{:S(2)}, u32[]{:S(2)}) collective-permute-start(bf16[96,1536]{1,0:T(8,128)(2,1)S(1)} %get-tuple-element.164), channel_id=1, source_target_pairs={{0,4},{2,6},{8,0},{10,2},{16,8},{18,10},{24,16},{26,18},{28,24},{3... | collective-permute-start | bytes 884744 | tf_op jit(solution)/shard_map/ppermute | solution.py:95
  133.9 18.9 %collective-permute-start.22 = (bf16[96,1536]{1,0:T(8,128)(2,1)S(1)}, bf16[96,1536]{1,0:T(8,128)(2,1)S(1)}, u32[]{:S(2)}, u32[]{:S(2)}) collective-permute-start(bf16[96,1536]{1,0:T(8,128)(2,1)S(1)} %get-tuple-element.165), channel_id=1, source_target_pairs={{0,8},{2,10},{8,16},{10,18},{16,24},{18,26},{24,28},{26,30},{28,20... | collective-permute-start | bytes 884744 | tf_op jit(solution)/shard_map/ppermute | solution.py:95
  134.7 15.5 %collective-permute-start.29 = (bf16[7,7,768]{2,1,0:T(8,128)(2,1)S(1)}, bf16[7,7,768]{2,1,0:T(8,128)(2,1)S(1)}, u32[]{:S(2)}, u32[]{:S(2)}) collective-permute-start(bf16[7,7,768]{2,1,0:T(8,128)(2,1)S(1)} %add_convert_fusion.31), channel_id=1, source_target_pairs={{0,4},{2,6},{4,0},{6,2},{8,12},{10,14},{12,8},{14,10},{16,20},{18,... | collective-permute-start | bytes 225800 | tf_op jit(solution)/shard_map/ppermute | solution.py:238
  137.4 51.1 %collective-permute-start.9 = (bf16[3,144,768]{2,1,0:T(8,128)(2,1)S(1)}, bf16[3,144,768]{2,1,0:T(8,128)(2,1)S(1)}, u32[]{:S(2)}, u32[]{:S(2)}) collective-permute-start(bf16[3,144,768]{2,1,0:T(8,128)(2,1)S(1)} %bitcast.33), channel_id=1, source_target_pairs={{2,0},{4,2},{6,4},{8,6},{10,8},{12,10},{14,12},{16,14},{18,16},{20... | collective-permute-start | bytes 1990664 | tf_op jit(solution)/shard_map/ppermute | solution.py:15
  138.7 51.8 %collective-permute-start.8 = (bf16[3,144,768]{2,1,0:T(8,128)(2,1)S(1)}, bf16[3,144,768]{2,1,0:T(8,128)(2,1)S(1)}, u32[]{:S(2)}, u32[]{:S(2)}) collective-permute-start(bf16[3,144,768]{2,1,0:T(8,128)(2,1)S(1)} %bitcast.34), channel_id=1, source_target_pairs={{0,2},{2,4},{4,6},{6,8},{8,10},{10,12},{12,14},{14,16},{16,18},{18... | collective-permute-start | bytes 1990664 | tf_op jit(solution)/shard_map/ppermute | solution.py:14
  150.2 12.5 %collective-permute-start.16 = (bf16[96,1536]{1,0:T(8,128)(2,1)S(1)}, bf16[96,1536]{1,0:T(8,128)(2,1)S(1)}, u32[]{:S(2)}, u32[]{:S(2)}) collective-permute-start(bf16[96,1536]{1,0:T(8,128)(2,1)S(1)} %get-tuple-element.26), channel_id=1, source_target_pairs={{0,8},{2,10},{8,16},{10,18},{16,24},{18,26},{24,28},{26,30},{28,20... | collective-permute-start | bytes 884744 | tf_op jit(solution)/shard_map/ppermute | solution.py:95
  150.2 12.6 %collective-permute-start.17 = (bf16[96,1536]{1,0:T(8,128)(2,1)S(1)}, bf16[96,1536]{1,0:T(8,128)(2,1)S(1)}, u32[]{:S(2)}, u32[]{:S(2)}) collective-permute-start(bf16[96,1536]{1,0:T(8,128)(2,1)S(1)} %get-tuple-element.27), channel_id=1, source_target_pairs={{0,4},{2,6},{8,0},{10,2},{16,8},{18,10},{24,16},{26,18},{28,24},{3... | collective-permute-start | bytes 884744 | tf_op jit(solution)/shard_map/ppermute | solution.py:95
  152.7 7.4 %collective-permute-start.32 = (bf16[7,7,768]{2,1,0:T(8,128)(2,1)S(1)}, bf16[7,7,768]{2,1,0:T(8,128)(2,1)S(1)}, u32[]{:S(2)}, u32[]{:S(2)}) collective-permute-start(bf16[7,7,768]{2,1,0:T(8,128)(2,1)S(1)} %add_convert_fusion.30), channel_id=1, source_target_pairs={{0,8},{2,10},{4,12},{6,14},{8,0},{10,2},{12,4},{14,6},{16,24},{18,... | collective-permute-start | bytes 225800 | tf_op jit(solution)/shard_map/ppermute | solution.py:238
  160.1 14.0 %collective-permute-start.27 = (bf16[96,1536]{1,0:T(8,128)(2,1)S(1)}, bf16[96,1536]{1,0:T(8,128)(2,1)S(1)}, u32[]{:S(2)}, u32[]{:S(2)}) collective-permute-start(bf16[96,1536]{1,0:T(8,128)(2,1)S(1)} %get-tuple-element.162), channel_id=1, source_target_pairs={{0,4},{2,6},{8,0},{10,2},{16,8},{18,10},{24,16},{26,18},{28,24},{3... | collective-permute-start | bytes 884744 | tf_op jit(solution)/shard_map/ppermute | solution.py:95
  162.7 15.0 %collective-permute-start.26 = (bf16[96,1536]{1,0:T(8,128)(2,1)S(1)}, bf16[96,1536]{1,0:T(8,128)(2,1)S(1)}, u32[]{:S(2)}, u32[]{:S(2)}) collective-permute-start(bf16[96,1536]{1,0:T(8,128)(2,1)S(1)} %get-tuple-element.163), channel_id=1, source_target_pairs={{0,8},{2,10},{8,16},{10,18},{16,24},{18,26},{24,28},{26,30},{28,20... | collective-permute-start | bytes 884744 | tf_op jit(solution)/shard_map/ppermute | solution.py:95
  162.8 7.1 %collective-permute-start.33 = (bf16[7,7,768]{2,1,0:T(8,128)(2,1)S(1)}, bf16[7,7,768]{2,1,0:T(8,128)(2,1)S(1)}, u32[]{:S(2)}, u32[]{:S(2)}) collective-permute-start(bf16[7,7,768]{2,1,0:T(8,128)(2,1)S(1)} %add_convert_fusion.29), channel_id=1, source_target_pairs={{0,16},{2,18},{4,20},{6,22},{8,24},{10,26},{12,28},{14,30},{16,0},... | collective-permute-start | bytes 225800 | tf_op jit(solution)/shard_map/ppermute | solution.py:238
  169.9 15.0 %collective-permute-start.37 = (bf16[96,1536]{1,0:T(8,128)(2,1)S(1)}, bf16[96,1536]{1,0:T(8,128)(2,1)S(1)}, u32[]{:S(2)}, u32[]{:S(2)}) collective-permute-start(bf16[96,1536]{1,0:T(8,128)(2,1)S(1)} %get-tuple-element.38), channel_id=1, source_target_pairs={{0,8},{2,10},{8,16},{10,18},{16,24},{18,26},{24,28},{26,30},{28,20... | collective-permute-start | bytes 884744 | tf_op jit(solution)/shard_map/ppermute | solution.py:95
  174.2 12.8 %collective-permute-start.38 = (bf16[96,1536]{1,0:T(8,128)(2,1)S(1)}, bf16[96,1536]{1,0:T(8,128)(2,1)S(1)}, u32[]{:S(2)}, u32[]{:S(2)}) collective-permute-start(bf16[96,1536]{1,0:T(8,128)(2,1)S(1)} %get-tuple-element.39), channel_id=1, source_target_pairs={{0,4},{2,6},{8,0},{10,2},{16,8},{18,10},{24,16},{26,18},{28,24},{3... | collective-permute-start | bytes 884744 | tf_op jit(solution)/shard_map/ppermute | solution.py:95
  178.9 23.1 %collective-permute-start.30 = (bf16[96,1536]{1,0:T(8,128)(2,1)S(1)}, bf16[96,1536]{1,0:T(8,128)(2,1)S(1)}, u32[]{:S(2)}, u32[]{:S(2)}) collective-permute-start(bf16[96,1536]{1,0:T(8,128)(2,1)S(1)} %get-tuple-element.32), channel_id=1, source_target_pairs={{0,8},{2,10},{8,16},{10,18},{16,24},{18,26},{24,28},{26,30},{28,20... | collective-permute-start | bytes 884744 | tf_op jit(solution)/shard_map/ppermute | solution.py:95
  185.0 17.1 %collective-permute-start.31 = (bf16[96,1536]{1,0:T(8,128)(2,1)S(1)}, bf16[96,1536]{1,0:T(8,128)(2,1)S(1)}, u32[]{:S(2)}, u32[]{:S(2)}) collective-permute-start(bf16[96,1536]{1,0:T(8,128)(2,1)S(1)} %get-tuple-element.33), channel_id=1, source_target_pairs={{0,4},{2,6},{8,0},{10,2},{16,8},{18,10},{24,16},{26,18},{28,24},{3... | collective-permute-start | bytes 884744 | tf_op jit(solution)/shard_map/ppermute | solution.py:95
  188.4 17.0 %collective-permute-start.39 = (bf16[96,1536]{1,0:T(8,128)(2,1)S(1)}, bf16[96,1536]{1,0:T(8,128)(2,1)S(1)}, u32[]{:S(2)}, u32[]{:S(2)}) collective-permute-start(bf16[96,1536]{1,0:T(8,128)(2,1)S(1)} %get-tuple-element.40), channel_id=1, source_target_pairs={{0,8},{2,10},{8,16},{10,18},{16,24},{18,26},{24,28},{26,30},{28,20... | collective-permute-start | bytes 884744 | tf_op jit(solution)/shard_map/ppermute | solution.py:95
  188.4 16.9 %collective-permute-start.40 = (bf16[96,1536]{1,0:T(8,128)(2,1)S(1)}, bf16[96,1536]{1,0:T(8,128)(2,1)S(1)}, u32[]{:S(2)}, u32[]{:S(2)}) collective-permute-start(bf16[96,1536]{1,0:T(8,128)(2,1)S(1)} %get-tuple-element.41), channel_id=1, source_target_pairs={{0,4},{2,6},{8,0},{10,2},{16,8},{18,10},{24,16},{26,18},{28,24},{3... | collective-permute-start | bytes 884744 | tf_op jit(solution)/shard_map/ppermute | solution.py:95
  203.3 6.8 %collective-permute-start.34 = (bf16[96,1536]{1,0:T(8,128)(2,1)S(1)}, bf16[96,1536]{1,0:T(8,128)(2,1)S(1)}, u32[]{:S(2)}, u32[]{:S(2)}) collective-permute-start(bf16[96,1536]{1,0:T(8,128)(2,1)S(1)} %get-tuple-element.36), channel_id=1, source_target_pairs={{0,8},{2,10},{8,16},{10,18},{16,24},{18,26},{24,28},{26,30},{28,20... | collective-permute-start | bytes 884744 | tf_op jit(solution)/shard_map/ppermute | solution.py:95
  203.4 6.7 %collective-permute-start.35 = (bf16[96,1536]{1,0:T(8,128)(2,1)S(1)}, bf16[96,1536]{1,0:T(8,128)(2,1)S(1)}, u32[]{:S(2)}, u32[]{:S(2)}) collective-permute-start(bf16[96,1536]{1,0:T(8,128)(2,1)S(1)} %get-tuple-element.37), channel_id=1, source_target_pairs={{0,4},{2,6},{8,0},{10,2},{16,8},{18,10},{24,16},{26,18},{28,24},{3... | collective-permute-start | bytes 884744 | tf_op jit(solution)/shard_map/ppermute | solution.py:95
  206.6 6.8 %collective-permute-start.41 = (bf16[96,1536]{1,0:T(8,128)(2,1)S(1)}, bf16[96,1536]{1,0:T(8,128)(2,1)S(1)}, u32[]{:S(2)}, u32[]{:S(2)}) collective-permute-start(bf16[96,1536]{1,0:T(8,128)(2,1)S(1)} %get-tuple-element.42), channel_id=1, source_target_pairs={{0,8},{2,10},{8,16},{10,18},{16,24},{18,26},{24,28},{26,30},{28,20... | collective-permute-start | bytes 884744 | tf_op jit(solution)/shard_map/ppermute | solution.py:95
  206.7 6.7 %collective-permute-start.42 = (bf16[96,1536]{1,0:T(8,128)(2,1)S(1)}, bf16[96,1536]{1,0:T(8,128)(2,1)S(1)}, u32[]{:S(2)}, u32[]{:S(2)}) collective-permute-start(bf16[96,1536]{1,0:T(8,128)(2,1)S(1)} %get-tuple-element.43), channel_id=1, source_target_pairs={{0,4},{2,6},{8,0},{10,2},{16,8},{18,10},{24,16},{26,18},{28,24},{3... | collective-permute-start | bytes 884744 | tf_op jit(solution)/shard_map/ppermute | solution.py:95
  211.4 3.4 %collective-permute-start.36 = (bf16[96,1536]{1,0:T(8,128)(2,1)S(1)}, bf16[96,1536]{1,0:T(8,128)(2,1)S(1)}, u32[]{:S(2)}, u32[]{:S(2)}) collective-permute-start(bf16[96,1536]{1,0:T(8,128)(2,1)S(1)} %get-tuple-element.151), channel_id=1, source_target_pairs={{0,2},{2,0},{4,6},{6,4},{8,10},{10,8},{12,14},{14,12},{16,18},{18,... | collective-permute-start | bytes 884744 | tf_op jit(solution)/shard_map/ppermute | solution.py:105
  214.6 1.6 collective-permute-start.43
  (62 other events, 264.7 us)
where the time goes:
time: 218 us; the launch traced here: 217 us
  starting transfers between devices  66.1 us (30%)
  other arithmetic  55 us (25%)
  waiting for transfers between devices  51.2 us (23%)
  matrix products  37.9 us (17%)
  local copies, waits for them, and re-layouts  4.82 us (2%)
  between operations  2.42 us (1%)
    ppermute x28, starting transfers between devices, ring_step(): got = lax.ppermute(sums[side], 'rows', ring_pairs(chips, way))  39.7 us
    ppermute x28, waiting for transfers between devices, ring_step(): got = lax.ppermute(sums[side], 'rows', ring_pairs(chips, way))  24.1 us
    ppermute x4, waiting for transfers between devices, shards(): lax.ppermute(kernel_sum, 'rows', [(i, i ^ span) for i in range(rows)])  20.5 us
    dot_general x2, matrix products, pixel_sum(): lax.dot_general(left, right, (((0,), (0,)), ((), ())), preferred_element_...  14.7 us
    convert_element_type x12, other arithmetic, ring_step(): result.append(total.astype(jnp.bfloat16))  12 us
    convert_element_type x1, other arithmetic, shards(): grad_feature = (cot_own + conv_back(tie(grad_pad, middle), kernel, height...  10.7 us
    dot_general x1, matrix products, shards(): hidden = jnp.dot(normed_both, in_part, preferred_element_type=jnp.float32)  10.2 us
    convert_element_type x1, other arithmetic, shards(): conv_local = conv_taps(padded, kernel, height, width).astype(jnp.bfloat16)  9.76 us
  transfers between devices with their start and end apart: 44, of which 17 were waited for; matrix products, arithmetic and copies ran while one was open for 34% of the time, Pallas kernels for 0%

commit v1 on v0

--- a/solution.py
+++ b/solution.py
@@ -16,13 +16,18 @@
     return above, below
 
 
-def conv_taps(padded, kernel, height, width):
-    result = jnp.zeros((height, width, kernel.shape[2]), jnp.float32)
-    for tap_row in range(7):
+def conv_line(cells, kernel, line, rim, height, width, begun):
+    own = range(3 - line, 3 - line + height)
+    if begun is None:
+        result = jnp.zeros((1, width, kernel.shape[2]), jnp.float32)
+        tap_rows = [tap for tap in range(7) if tap in own]
+    else:
+        result = begun
+        tap_rows = [tap for tap in range(7) if tap not in own]
+    for tap_row in tap_rows:
+        row = line + tap_row - 3 + rim
         for tap_col in range(7):
-            window = padded[tap_row : tap_row + height, tap_col : tap_col + width].astype(
-                jnp.float32
-            )
+            window = cells[row : row + 1, tap_col : tap_col + width].astype(jnp.float32)
             result = result + window * kernel[tap_row, tap_col]
     return result
 
@@ -137,9 +142,15 @@
     grad_activ = lax.dot_general(
         mixed_both, out_part, (((1,), (1,)), ((), ())), preferred_element_type=jnp.float32
     )
+    inner = jnp.pad(feature, ((0, 0), (3, 3), (0, 0)))
+    begun = [conv_line(inner, kernel, line, 0, height, width, None) for line in range(height)]
+    above, below, begun = lax.optimization_barrier((above, below, begun))
     rimmed = jnp.concatenate([above, feature, below], axis=0)
     padded = jnp.pad(rimmed, ((0, 0), (3, 3), (0, 0)))
-    conv_local = conv_taps(padded, kernel, height, width).astype(jnp.bfloat16)
+    lines = [
+        conv_line(padded, kernel, line, 3, height, width, begun[line]) for line in range(height)
+    ]
+    conv_local = jnp.concatenate(lines, axis=0).astype(jnp.bfloat16)
     conv_local = conv_local.reshape(pixels, local_ch)
     if chan == 2:
         conv_other = lax.ppermute(conv_local, "chan", cross)
@@ -214,6 +225,15 @@
             jnp.bfloat16
         )
 
+    def spread(summed, span):
+        width_of = min(4, rows // span)
+        total = summed.astype(jnp.float32)
+        for other in range(1, width_of):
+            pairs = [(i, i ^ (span * other)) for i in range(rows)]
+            total = total + lax.ppermute(summed, "rows", pairs).astype(jnp.float32)
+        span *= width_of
+        return (total if span >= rows else total.astype(jnp.bfloat16)), span
+
     kernel_sum = None
     grad_feature = None
     span = 1
@@ -229,27 +249,22 @@
             if step == 4 and which == 0:
                 kernel_sum = terms(tie(grad_conv, early), range(7))
                 sums[which] = tie(sums[which], kernel_sum)
+            if step == 5 and which == 1:
+                kernel_sum, span = spread(kernel_sum, span)
+                sums[which] = tie(sums[which], kernel_sum)
             if step == last and which == 1:
                 grad_feature = (
                     cot_own + conv_back(tie(grad_pad, middle), kernel, height, width)
                 ).astype(jnp.bfloat16)
                 sums[which] = tie(sums[which], grad_feature)
-            if step > 4 and span < rows:
-                other = lax.ppermute(kernel_sum, "rows", [(i, i ^ span) for i in range(rows)])
-                total = kernel_sum.astype(jnp.float32) + other.astype(jnp.float32)
-                span *= 2
-                kernel_sum = total if span >= rows else total.astype(jnp.bfloat16)
-                sums[which] = tie(sums[which], kernel_sum)
             sums[which] = ring_step(totals[which], sums[which], step, place, chips)
         if step == 1:
             early = list(sums)
         if step == 3:
             middle = list(sums)
     while span < rows:
-        other = lax.ppermute(kernel_sum, "rows", [(i, i ^ span) for i in range(rows)])
-        total = kernel_sum.astype(jnp.float32) + other.astype(jnp.float32)
-        span *= 2
-        kernel_sum = total if span >= rows else total.astype(jnp.bfloat16)
+        kernel_sum, span = spread(kernel_sum, span)
+    sums[1] = tie(sums[1], kernel_sum)
     grad_w_out = own_rows(sums[0], core, swap).T
     grad_w_in = own_rows(sums[1], core, swap)
     return (grad_feature, grad_w_in, grad_w_out, kernel_sum)

time: 218 us -> 231 us (1.060); the launches traced: 217 us -> 227 us
  waiting for transfers between devices: 51.2 us -> 65.3 us
  starting transfers between devices: 66.1 us -> 54.1 us
  other arithmetic: 55 us -> 58 us
  matrix products: 37.9 us -> 40.4 us
    ppermute x28, waiting for transfers between devices: 24.1 us -> 49.4 us  [ring_step(): got = lax.ppermute(sums[side], 'rows', ring_pairs(chips, way))]
    ppermute x4 -> x6, waiting for transfers between devices: 20.5 us -> 8.49 us  [spread(): total = total + lax.ppermute(summed, 'rows', pairs).astype(jnp.float32)]
    convert_element_type x4 -> x1, other arithmetic: 9.83 us -> 0.05 us  [spread(): return (total if span >= rows else total.astype(jnp.bfloat16), span)]
    ppermute x28, starting transfers between devices: 39.7 us -> 31.2 us  [ring_step(): got = lax.ppermute(sums[side], 'rows', ring_pairs(chips, way))]
    another operation x0 -> x3, other arithmetic: none -> 8.06 us
    ppermute x1, starting transfers between devices: 9.57 us -> 2.9 us  [shards(): lax.ppermute(normed, 'rows', swap)]
    ppermute x4 -> x6, starting transfers between devices: 1.49 us -> 6.38 us  [spread(): total = total + lax.ppermute(summed, 'rows', pairs).astype(jnp.float32)]
    add x1 -> x4, other arithmetic: 0.69 us -> 4.93 us  [the longest x3 4.22 us: conv_line(): result = result + window * kernel[tap_row, tap_col]]
  transfers between devices with their start and end apart: 44 -> 46, of which waited for: 17 -> 25; matrix products, arithmetic and copies ran while one was open for 34% -> 35% of each run, Pallas kernels for 0% -> 0%
where the time goes in v1:
time: 231 us; the launch traced here: 227 us
  waiting for transfers between devices  65.3 us (28%)
  other arithmetic  58 us (25%)
  starting transfers between devices  54.1 us (23%)
  matrix products  40.4 us (17%)
  local copies, waits for them, and re-layouts  6.05 us (3%)
  between operations  2.74 us (1%)
    ppermute x28, waiting for transfers between devices, ring_step(): got = lax.ppermute(sums[side], 'rows', ring_pairs(chips, way))  49.4 us
    ppermute x28, starting transfers between devices, ring_step(): got = lax.ppermute(sums[side], 'rows', ring_pairs(chips, way))  31.2 us
    dot_general x2, matrix products, pixel_sum(): lax.dot_general(left, right, (((0,), (0,)), ((), ())), preferred_element_...  15.7 us
    convert_element_type x12, other arithmetic, ring_step(): result.append(total.astype(jnp.bfloat16))  12.5 us
    dot_general x1, matrix products, shards(): hidden = jnp.dot(normed_both, in_part, preferred_element_type=jnp.float32)  11.7 us
    convert_element_type x1, other arithmetic, shards(): grad_feature = (cot_own + conv_back(tie(grad_pad, middle), kernel, height...  10.7 us
    reduce_sum x3, other arithmetic, kernel_terms(): cols_list.append(jnp.sum(grad_float * window, axis=(0, 1)))  9.55 us
    ppermute x6, waiting for transfers between devices, spread(): total = total + lax.ppermute(summed, 'rows', pairs).astype(jnp.float32)  8.49 us
  transfers between devices with their start and end apart: 46, of which 25 were waited for; matrix products, arithmetic and copies ran while one was open for 35% of the time, Pallas kernels for 0%

profile of v1, /device:TPU:0, one launch (start us, length us, event | category | flops | bytes accessed | tf_op | source)
XLA Modules:
  0.0 226.6 jit_solution(13585694077153298661)
XLA Ops:
  0.7 2.5 %collective-permute-start = (bf16[3,144,768]{2,1,0:T(8,128)(2,1)}, bf16[3,144,768]{2,1,0:T(8,128)(2,1)S(1)}, u32[]{:S(2)}, u32[]{:S(2)}) collective-permute-start(bf16[3,144,768]{2,1,0:T(8,128)(2,1)} %param.7), channel_id=1, source_target_pairs={{0,2},{2,4},{4,6},{6,8},{8,10},{10,12},{12,14},{14,16},{16,18},{18... | collective-permute-start | bytes 1990664 | tf_op jit(solution)/shard_map/ppermute | solution.py:14
  4.5 2.6 %fusion.28 = bf16[432,1536]{1,0:T(8,128)(2,1)} fusion(bf16[3,144,1536]{2,1,0:T(8,128)(2,1)} %param.13, f32[1536]{0:T(1024)} %param.10), kind=kLoop, calls=%fused_computation.87 | loop fusion | flops 1990656 | bytes 2660352 | tf_op jit(solution)/shard_map/convert_element_type | solution.py:136
  7.1 3.2 %collective-permute-start.3 = (bf16[432,1536]{1,0:T(8,128)(2,1)}, bf16[432,1536]{1,0:T(8,128)(2,1)}, u32[]{:S(2)}, u32[]{:S(2)}) collective-permute-start(bf16[432,1536]{1,0:T(8,128)(2,1)} %fusion.28), channel_id=1, source_target_pairs={{0,2},{2,0},{4,6},{6,4},{8,10},{10,8},{12,14},{14,12},{16,18},{18,... | collective-permute-start | bytes 3981320 | tf_op jit(solution)/shard_map/ppermute | solution.py:139
  12.3 1.9 fusion.211
  16.8 2.2 fusion.37
  19.2 2.7 %fusion.227 = bf16[1,144,768]{2,1,0:T(8,128)(2,1)S(1)} fusion(f32[1,144,768]{2,1,0:T(8,128)S(1)} %fusion.171, bf16[9,150,768]{2,1,0:T(8,128)(2,1)S(1)} %fusion.37, f32[768]{0:T(1024)S(1)} %copy-done.52, f32[768]{0:T(1024)S(1)} %copy-done.50, f32[768]{0:T(1024)S(1)} %copy-done.28, f32[768]{0:T(1024)S(1)} %copy-done.30, f32[768]{0:T(1024)S(1)} %copy-done.32, ...), kind=kLoop, calls=%fused_computation.460 | loop fusion | flops 9400320 | bytes 6942720 | tf_op jit(solution)/shard_map/convert.2
  21.9 2.7 %fusion.151 = bf16[1,144,768]{2,1,0:T(8,128)(2,1)S(1)} fusion(f32[1,144,768]{2,1,0:T(8,128)S(1)} %fusion.191, f32[768]{0:T(1024)S(1)} %copy-done.52, f32[768]{0:T(1024)S(1)} %copy-done.50, f32[768]{0:T(1024)S(1)} %copy-done.28, f32[768]{0:T(1024)S(1)} %copy-done.30, f32[768]{0:T(1024)S(1)} %copy-done.32, f32[768]{0:T(1024)S(1)} %copy-done.34, ...), kind=kLoop, calls=%fused_computation.384 | loop fusion | flops 9400320 | bytes 6942720 | tf_op jit(solution)/shard_map/convert.3
  24.6 2.7 %fusion.226 = bf16[1,144,768]{2,1,0:T(8,128)(2,1)S(1)} fusion(f32[1,144,768]{2,1,0:T(8,128)S(1)} %copy-done.12, bf16[9,150,768]{2,1,0:T(8,128)(2,1)S(1)} %fusion.37, bf16[3,144,768]{2,1,0:T(8,128)(2,1)} %collective-permute-done.1, f32[768]{0:T(1024)S(1)} %copy-done.52, f32[768]{0:T(1024)S(1)} %copy-done.50, f32[768]{0:T(1024)S(1)} %copy-done.28, ...), kind=kLoop, calls=%fused_computation.459 | loop fusion | flops 9400320 | bytes 6942720 | tf_op jit(solution)/shard_map/convert.4
  27.4 1.6 collective-permute-start.2
  29.1 7.9 %fusion.9 = f32[864,1536]{1,0:T(8,128)} fusion(bf16[3072,1536]{1,0:T(8,128)(2,1)S(1)} %bitcast.44, s32[]{:T(128)S(6)} %select_n.194, bf16[432,1536]{1,0:T(8,128)(2,1)} %collective-permute-done.3, bf16[432,1536]{1,0:T(8,128)(2,1)} %fusion.28), kind=kOutput, calls=%fused_computation.65 | convolution fusion | flops 4082171904 | bytes 12681220 | tf_op jit(solution)/shard_map/dot_general | solution.py:142
  36.9 5.3 %collective-permute-done.2 = bf16[432,768]{1,0:T(8,128)(2,1)S(1)} collective-permute-done((bf16[432,768]{1,0:T(8,128)(2,1)S(1)}, bf16[432,768]{1,0:T(8,128)(2,1)S(1)}, u32[]{:S(2)}, u32[]{:S(2)}) %collective-permute-start.2) | collective-permute-done | bytes 663584 | tf_op jit(solution)/shard_map/ppermute | solution.py:156
  43.4 1.6 fusion.25
  45.0 2.9 %collective-permute-start.4 = (bf16[432,1536]{1,0:T(8,128)(2,1)}, bf16[432,1536]{1,0:T(8,128)(2,1)}, u32[]{:S(2)}, u32[]{:S(2)}) collective-permute-start(bf16[432,1536]{1,0:T(8,128)(2,1)} %fusion.25), channel_id=1, source_target_pairs={{0,2},{2,0},{4,6},{6,4},{8,10},{10,8},{12,14},{14,12},{16,18},{18,... | collective-permute-start | bytes 3981320 | tf_op jit(solution)/shard_map/ppermute | solution.py:174
  50.9 11.7 %fusion.8 = (bf16[864,1536]{1,0:T(8,128)(2,1)S(1)}, f32[864,1536]{1,0:T(8,128)}) fusion(f32[864,1536]{1,0:T(8,128)} %fusion.9, bf16[1536,3072]{1,0:T(8,128)(2,1)} %param.11, s32[]{:T(128)S(6)} %select_n.194, bf16[432,1536]{1,0:T(8,128)(2,1)} %collective-permute-done.4, bf16[432,1536]{1,0:T(8,128)(2,1)} %fusion.25), kind=kOutput, calls=%fused_computation.63 | convolution fusion | flops 4108713984 | bytes 20643844 | tf_op jit(solution)/shard_map/dot_general | solution.py:175
  62.8 7.5 %fusion = bf16[1536,1536]{1,0:T(8,128)(2,1)S(1)} fusion(bf16[864,1536]{1,0:T(8,128)(2,1)S(1)} %get-tuple-element.193, bf16[432,1536]{1,0:T(8,128)(2,1)} %collective-permute-done.4, bf16[432,1536]{1,0:T(8,128)(2,1)} %fusion.25), kind=kOutput, calls=%fused_computation.53 | convolution fusion | flops 4086890496 | bytes 10027008 | tf_op jit(solution)/shard_map/dot_general | solution.py:180
  70.3 2.7 %collective-permute-start.18 = (bf16[96,1536]{1,0:T(8,128)(2,1)S(1)}, bf16[96,1536]{1,0:T(8,128)(2,1)S(1)}, u32[]{:S(2)}, u32[]{:S(2)}) collective-permute-start(bf16[96,1536]{1,0:T(8,128)(2,1)S(1)} %get-tuple-element.172), channel_id=1, source_target_pairs={{0,8},{2,10},{8,16},{10,18},{16,24},{18,26},{24,28},{26,30},{28,20... | collective-permute-start | bytes 884744 | tf_op jit(solution)/shard_map/ppermute | solution.py:100
  73.7 8.2 %fusion.1 = bf16[1536,1536]{1,0:T(8,128)(2,1)S(1)} fusion(f32[864,1536]{1,0:T(8,128)} %get-tuple-element.194, bf16[432,1536]{1,0:T(8,128)(2,1)} %collective-permute-done.3, bf16[432,1536]{1,0:T(8,128)(2,1)} %fusion.28), kind=kOutput, calls=%fused_computation.54 | convolution fusion | flops 4098834432 | bytes 12681216 | tf_op jit(solution)/shard_map/dot_general | solution.py:180
  84.1 2.3 fusion.22
  86.4 4.4 %collective-permute-done.10 = bf16[96,1536]{1,0:T(8,128)(2,1)S(1)} collective-permute-done((bf16[96,1536]{1,0:T(8,128)(2,1)S(1)}, bf16[96,1536]{1,0:T(8,128)(2,1)S(1)}, u32[]{:S(2)}, u32[]{:S(2)}) %collective-permute-start.10) | collective-permute-done | bytes 294944 | tf_op jit(solution)/shard_map/ppermute | solution.py:100
  92.0 1.6 collective-permute-start.11
  94.3 5.2 %collective-permute-done.11 = bf16[96,1536]{1,0:T(8,128)(2,1)S(1)} collective-permute-done((bf16[96,1536]{1,0:T(8,128)(2,1)S(1)}, bf16[96,1536]{1,0:T(8,128)(2,1)S(1)}, u32[]{:S(2)}, u32[]{:S(2)}) %collective-permute-start.11) | collective-permute-done | bytes 294944 | tf_op jit(solution)/shard_map/ppermute | solution.py:100
  101.8 1.6 collective-permute-start.12
  103.9 2.8 %multiply_reduce_fusion = (f32[432]{0:T(512)S(1)}, f32[432]{0:T(512)S(1)}, f32[432,1536]{1,0:T(8,128)S(1)}) fusion(f32[1536]{0:T(1024)S(1)} %copy-done.57, f32[432]{0:T(512)S(1)} %copy-done.59, f32[432]{0:T(512)S(1)} %copy-done.55, bf16[432,768]{1,0:T(8,128)(2,1)S(1)} %copy-done.6, bf16[432,768]{1,0:T(8,128)(2,1)S(1)} %copy-done.4, ...), kind=kOutput, calls=%fused_computation.93 | convolution fusion | flops 2046393600 | bytes 11369860 | tf_op jit(solution)/shard_map/dot_general | solution.py:186
  106.8 1.6 collective-permute-start.7
  109.0 1.6 collective-permute-start.20
  111.1 4.7 %collective-permute-done.20 = bf16[96,1536]{1,0:T(8,128)(2,1)S(1)} collective-permute-done((bf16[96,1536]{1,0:T(8,128)(2,1)S(1)}, bf16[96,1536]{1,0:T(8,128)(2,1)S(1)}, u32[]{:S(2)}, u32[]{:S(2)}) %collective-permute-start.20) | collective-permute-done | bytes 294944 | tf_op jit(solution)/shard_map/ppermute | solution.py:100
  115.7 1.6 collective-permute-done.23
  122.4 3.2 %fusion.85 = (f32[768]{0:T(1024)S(1)}, f32[768]{0:T(1024)S(1)}, f32[768]{0:T(1024)S(1)}, f32[768]{0:T(1024)S(1)}, f32[768]{0:T(1024)S(1)}, /*index=5*/f32[768]{0...) fusion(bf16[3,144,768]{2,1,0:T(8,128)(2,1)S(1)} %bitcast.30, ...), kind=kLoop, calls=%fused_computation.148 | loop fusion | flops 18233856 | bytes 12662784 | tf_op jit(solution)/shard_map/reduce_sum | solution.py:55
  125.7 3.3 %fusion.86 = (f32[768]{0:T(1024)S(1)}, f32[768]{0:T(1024)S(1)}, f32[768]{0:T(1024)S(1)}, f32[768]{0:T(1024)S(1)}, f32[768]{0:T(1024)S(1)}, /*index=5*/f32[768]{0...) fusion(bf16[3,144,768]{2,1,0:T(8,128)(2,1)S(1)} %bitcast.31, ...), kind=kLoop, calls=%fused_computation.149 | loop fusion | flops 18233856 | bytes 12662784 | tf_op jit(solution)/shard_map/reduce_sum | solution.py:55
  129.0 3.0 %fusion.84 = (f32[768]{0:T(1024)S(1)}, f32[768]{0:T(1024)S(1)}, f32[768]{0:T(1024)S(1)}, f32[768]{0:T(1024)S(1)}, f32[768]{0:T(1024)S(1)}, /*index=5*/f32[768]{0...) fusion(bf16[3,144,768]{2,1,0:T(8,128)(2,1)S(1)} %bitcast.32, ...), kind=kLoop, calls=%fused_computation.147 | loop fusion | flops 13261056 | bytes 9329664 | tf_op jit(solution)/shard_map/reduce_sum | solution.py:55
  136.4 1.7 collective-permute-start.22
  139.5 1.7 collective-permute-start.35
  145.4 4.5 %collective-permute-done.35 = bf16[7,7,768]{2,1,0:T(8,128)(2,1)S(1)} collective-permute-done((bf16[7,7,768]{2,1,0:T(8,128)(2,1)S(1)}, bf16[7,7,768]{2,1,0:T(8,128)(2,1)S(1)}, u32[]{:S(2)}, u32[]{:S(2)}) %collective-permute-start.35) | collective-permute-done | bytes 75296 | tf_op jit(solution)/shard_map/ppermute | solution.py:233
  151.2 3.0 %collective-permute-done.36 = bf16[7,7,768]{2,1,0:T(8,128)(2,1)S(1)} collective-permute-done((bf16[7,7,768]{2,1,0:T(8,128)(2,1)S(1)}, bf16[7,7,768]{2,1,0:T(8,128)(2,1)S(1)}, u32[]{:S(2)}, u32[]{:S(2)}) %collective-permute-start.36) | collective-permute-done | bytes 75296 | tf_op jit(solution)/shard_map/ppermute | solution.py:233
  159.5 1.6 collective-permute-start.26
  161.1 12.3 %collective-permute-done.16 = bf16[96,1536]{1,0:T(8,128)(2,1)S(1)} collective-permute-done((bf16[96,1536]{1,0:T(8,128)(2,1)S(1)}, bf16[96,1536]{1,0:T(8,128)(2,1)S(1)}, u32[]{:S(2)}, u32[]{:S(2)}) %collective-permute-start.16) | collective-permute-done | bytes 294944 | tf_op jit(solution)/shard_map/ppermute | solution.py:100
  175.5 4.3 %collective-permute-start.39 = (bf16[96,1536]{1,0:T(8,128)(2,1)S(1)}, bf16[96,1536]{1,0:T(8,128)(2,1)S(1)}, u32[]{:S(2)}, u32[]{:S(2)}) collective-permute-start(bf16[96,1536]{1,0:T(8,128)(2,1)S(1)} %get-tuple-element.44), channel_id=1, source_target_pairs={{0,8},{2,10},{8,16},{10,18},{16,24},{18,26},{24,28},{26,30},{28,20... | collective-permute-start | bytes 884744 | tf_op jit(solution)/shard_map/ppermute | solution.py:100
  179.8 3.2 %collective-permute-done.27 = bf16[96,1536]{1,0:T(8,128)(2,1)S(1)} collective-permute-done((bf16[96,1536]{1,0:T(8,128)(2,1)S(1)}, bf16[96,1536]{1,0:T(8,128)(2,1)S(1)}, u32[]{:S(2)}, u32[]{:S(2)}) %collective-permute-start.27) | collective-permute-done | bytes 294944 | tf_op jit(solution)/shard_map/ppermute | solution.py:100
  186.3 2.8 %collective-permute-done.42 = bf16[96,1536]{1,0:T(8,128)(2,1)S(1)} collective-permute-done((bf16[96,1536]{1,0:T(8,128)(2,1)S(1)}, bf16[96,1536]{1,0:T(8,128)(2,1)S(1)}, u32[]{:S(2)}, u32[]{:S(2)}) %collective-permute-start.42) | collective-permute-done | bytes 294944 | tf_op jit(solution)/shard_map/ppermute | solution.py:100
  190.3 1.7 collective-permute-start.40
  193.9 1.7 collective-permute-done.32
  195.6 1.7 collective-permute-done.40
  197.3 1.8 collective-permute-done.43
  200.7 1.8 collective-permute-start.41
  202.9 10.7 %add_convert_fusion = bf16[3,144,768]{2,1,0:T(8,128)(2,1)} fusion(f32[768]{0:T(1024)S(1)} %copy-done.53, bf16[9,150,768]{2,1,0:T(8,128)(2,1)S(1)} %select_maximum_fusion, f32[768]{0:T(1024)S(1)} %copy-done.51, f32[768]{0:T(1024)S(1)} %copy-done.29, f32[768]{0:T(1024)S(1)} %copy-done.31, f32[768]{0:T(1024)S(1)} %copy-done.33, f32[768]{0:T(1024)S(1)} %copy-done.35, ...), kind=kLoop, calls=%fused_computation.152 | loop fusion | flops 49434624 | bytes 33991684 | tf_op jit(solution)/shard_map/convert_element_type | solution.py:258
  213.6 1.8 collective-permute-start.33
  217.0 3.4 %collective-permute-done.33 = bf16[96,1536]{1,0:T(8,128)(2,1)S(1)} collective-permute-done((bf16[96,1536]{1,0:T(8,128)(2,1)S(1)}, bf16[96,1536]{1,0:T(8,128)(2,1)S(1)}, u32[]{:S(2)}, u32[]{:S(2)}) %collective-permute-start.33) | collective-permute-done | bytes 294944 | tf_op jit(solution)/shard_map/ppermute | solution.py:100
  220.4 1.8 collective-permute-done.34
  (305 shorter events, 55.6 us)
Async XLA Ops:
  0.7 16.1 %collective-permute-start = (bf16[3,144,768]{2,1,0:T(8,128)(2,1)}, bf16[3,144,768]{2,1,0:T(8,128)(2,1)S(1)}, u32[]{:S(2)}, u32[]{:S(2)}) collective-permute-start(bf16[3,144,768]{2,1,0:T(8,128)(2,1)} %param.7), channel_id=1, source_target_pairs={{0,2},{2,4},{4,6},{6,8},{8,10},{10,12},{12,14},{14,16},{16,18},{18... | collective-permute-start | bytes 1990664 | tf_op jit(solution)/shard_map/ppermute | solution.py:14
  3.2 13.6 %collective-permute-start.1 = (bf16[3,144,768]{2,1,0:T(8,128)(2,1)}, bf16[3,144,768]{2,1,0:T(8,128)(2,1)}, u32[]{:S(2)}, u32[]{:S(2)}) collective-permute-start(bf16[3,144,768]{2,1,0:T(8,128)(2,1)} %param.7), channel_id=1, source_target_pairs={{2,0},{4,2},{6,4},{8,6},{10,8},{12,10},{14,12},{16,14},{18,16},{20... | collective-permute-start | bytes 1990664 | tf_op jit(solution)/shard_map/ppermute | solution.py:15
  7.1 21.9 %collective-permute-start.3 = (bf16[432,1536]{1,0:T(8,128)(2,1)}, bf16[432,1536]{1,0:T(8,128)(2,1)}, u32[]{:S(2)}, u32[]{:S(2)}) collective-permute-start(bf16[432,1536]{1,0:T(8,128)(2,1)} %fusion.28), channel_id=1, source_target_pairs={{0,2},{2,0},{4,6},{6,4},{8,10},{10,8},{12,14},{14,12},{16,18},{18,... | collective-permute-start | bytes 3981320 | tf_op jit(solution)/shard_map/ppermute | solution.py:139
  16.8 32.5 %copy-start.1 = (bf16[3,144,768]{2,1,0:T(8,128)(2,1)}, bf16[3,144,768]{2,1,0:T(8,128)(2,1)S(1)}, u32[]{:S(2)}) copy-start(bf16[3,144,768]{2,1,0:T(8,128)(2,1)S(1)} %collective-permute-done) | copy-start | bytes 1990660
  27.4 14.8 %collective-permute-start.2 = (bf16[432,768]{1,0:T(8,128)(2,1)S(1)}, bf16[432,768]{1,0:T(8,128)(2,1)S(1)}, u32[]{:S(2)}, u32[]{:S(2)}) collective-permute-start(bf16[432,768]{1,0:T(8,128)(2,1)S(1)} %bitcast.36), channel_id=1, source_target_pairs={{0,1},{1,0},{2,3},{3,2},{4,5},{5,4},{6,7},{7,6},{8,9},{9,8},{10,11... | collective-permute-start | bytes 1990664 | tf_op jit(solution)/shard_map/ppermute | solution.py:156
  45.0 5.9 %collective-permute-start.4 = (bf16[432,1536]{1,0:T(8,128)(2,1)}, bf16[432,1536]{1,0:T(8,128)(2,1)}, u32[]{:S(2)}, u32[]{:S(2)}) collective-permute-start(bf16[432,1536]{1,0:T(8,128)(2,1)} %fusion.25), channel_id=1, source_target_pairs={{0,2},{2,0},{4,6},{6,4},{8,10},{10,8},{12,14},{14,12},{16,18},{18,... | collective-permute-start | bytes 3981320 | tf_op jit(solution)/shard_map/ppermute | solution.py:174
  70.3 47.0 %copy-start.9 = (bf16[1536,1536]{1,0:T(8,128)(2,1)}, bf16[1536,1536]{1,0:T(8,128)(2,1)S(1)}, u32[]{:S(2)}) copy-start(bf16[1536,1536]{1,0:T(8,128)(2,1)S(1)} %fusion) | copy-start | bytes 14155780
  70.3 23.7 %collective-permute-start.18 = (bf16[96,1536]{1,0:T(8,128)(2,1)S(1)}, bf16[96,1536]{1,0:T(8,128)(2,1)S(1)}, u32[]{:S(2)}, u32[]{:S(2)}) collective-permute-start(bf16[96,1536]{1,0:T(8,128)(2,1)S(1)} %get-tuple-element.172), channel_id=1, source_target_pairs={{0,8},{2,10},{8,16},{10,18},{16,24},{18,26},{24,28},{26,30},{28,20... | collective-permute-start | bytes 884744 | tf_op jit(solution)/shard_map/ppermute | solution.py:100
  73.0 21.1 %collective-permute-start.19 = (bf16[96,1536]{1,0:T(8,128)(2,1)S(1)}, bf16[96,1536]{1,0:T(8,128)(2,1)S(1)}, u32[]{:S(2)}, u32[]{:S(2)}) collective-permute-start(bf16[96,1536]{1,0:T(8,128)(2,1)S(1)} %get-tuple-element.171), channel_id=1, source_target_pairs={{0,4},{2,6},{8,0},{10,2},{16,8},{18,10},{24,16},{26,18},{28,24},{3... | collective-permute-start | bytes 884744 | tf_op jit(solution)/shard_map/ppermute | solution.py:100
  82.0 8.8 %collective-permute-start.10 = (bf16[96,1536]{1,0:T(8,128)(2,1)S(1)}, bf16[96,1536]{1,0:T(8,128)(2,1)S(1)}, u32[]{:S(2)}, u32[]{:S(2)}) collective-permute-start(bf16[96,1536]{1,0:T(8,128)(2,1)S(1)} %get-tuple-element.182), channel_id=1, source_target_pairs={{0,8},{2,10},{8,16},{10,18},{16,24},{18,26},{24,28},{26,30},{28,20... | collective-permute-start | bytes 884744 | tf_op jit(solution)/shard_map/ppermute | solution.py:100
  83.4 8.4 %collective-permute-start.13 = (bf16[96,1536]{1,0:T(8,128)(2,1)S(1)}, bf16[96,1536]{1,0:T(8,128)(2,1)S(1)}, u32[]{:S(2)}, u32[]{:S(2)}) collective-permute-start(bf16[96,1536]{1,0:T(8,128)(2,1)S(1)} %get-tuple-element.181), channel_id=1, source_target_pairs={{0,4},{2,6},{8,0},{10,2},{16,8},{18,10},{24,16},{26,18},{28,24},{3... | collective-permute-start | bytes 884744 | tf_op jit(solution)/shard_map/ppermute | solution.py:100
  86.3 17.6 %collective-permute-start.5 = (bf16[432,1536]{1,0:T(8,128)(2,1)S(1)}, bf16[432,1536]{1,0:T(8,128)(2,1)S(1)}, u32[]{:S(2)}, u32[]{:S(2)}) collective-permute-start(bf16[432,1536]{1,0:T(8,128)(2,1)S(1)} %fusion.22), channel_id=1, source_target_pairs={{0,2},{2,0},{4,6},{6,4},{8,10},{10,8},{12,14},{14,12},{16,18},{18,... | collective-permute-start | bytes 3981320 | tf_op jit(solution)/shard_map/ppermute | solution.py:191
  92.0 7.5 %collective-permute-start.11 = (bf16[96,1536]{1,0:T(8,128)(2,1)S(1)}, bf16[96,1536]{1,0:T(8,128)(2,1)S(1)}, u32[]{:S(2)}, u32[]{:S(2)}) collective-permute-start(bf16[96,1536]{1,0:T(8,128)(2,1)S(1)} %get-tuple-element.180), channel_id=1, source_target_pairs={{0,8},{2,10},{8,16},{10,18},{16,24},{18,26},{24,28},{26,30},{28,20... | collective-permute-start | bytes 884744 | tf_op jit(solution)/shard_map/ppermute | solution.py:100
  93.6 7.2 %collective-permute-start.14 = (bf16[96,1536]{1,0:T(8,128)(2,1)S(1)}, bf16[96,1536]{1,0:T(8,128)(2,1)S(1)}, u32[]{:S(2)}, u32[]{:S(2)}) collective-permute-start(bf16[96,1536]{1,0:T(8,128)(2,1)S(1)} %get-tuple-element.179), channel_id=1, source_target_pairs={{0,4},{2,6},{8,0},{10,2},{16,8},{18,10},{24,16},{26,18},{28,24},{3... | collective-permute-start | bytes 884744 | tf_op jit(solution)/shard_map/ppermute | solution.py:100
  101.8 39.4 %collective-permute-start.12 = (bf16[96,1536]{1,0:T(8,128)(2,1)}, bf16[96,1536]{1,0:T(8,128)(2,1)}, u32[]{:S(2)}, u32[]{:S(2)}) collective-permute-start(bf16[96,1536]{1,0:T(8,128)(2,1)} %get-tuple-element.178), channel_id=1, source_target_pairs={{0,8},{2,10},{8,16},{10,18},{16,24},{18,26},{24,28},{26,30},{28,20... | collective-permute-start | bytes 884744 | tf_op jit(solution)/shard_map/ppermute | solution.py:100
  103.4 39.2 %collective-permute-start.15 = (bf16[96,1536]{1,0:T(8,128)(2,1)}, bf16[96,1536]{1,0:T(8,128)(2,1)}, u32[]{:S(2)}, u32[]{:S(2)}) collective-permute-start(bf16[96,1536]{1,0:T(8,128)(2,1)} %get-tuple-element.177), channel_id=1, source_target_pairs={{0,4},{2,6},{8,0},{10,2},{16,8},{18,10},{24,16},{26,18},{28,24},{3... | collective-permute-start | bytes 884744 | tf_op jit(solution)/shard_map/ppermute | solution.py:100
  106.8 3.8 %collective-permute-start.7 = (f32[2,432]{1,0:T(2,128)S(1)}, f32[2,432]{1,0:T(2,128)S(1)}, u32[]{:S(2)}, u32[]{:S(2)}) collective-permute-start(f32[2,432]{1,0:T(2,128)S(1)} %pad_maximum_fusion.8), channel_id=1, source_target_pairs={{0,1},{1,0},{2,3},{3,2},{4,5},{5,4},{6,7},{7,6},{8,9},{9,8},{10,11... | collective-permute-start | bytes 10376 | tf_op jit(solution)/shard_map/ppermute | solution.py:205
  108.4 13.5 %collective-permute-start.6 = (bf16[432,768]{1,0:T(8,128)(2,1)S(1)}, bf16[432,768]{1,0:T(8,128)(2,1)S(1)}, u32[]{:S(2)}, u32[]{:S(2)}) collective-permute-start(bf16[432,768]{1,0:T(8,128)(2,1)S(1)} %dynamic-slice_convert_fusion), channel_id=1, source_target_pairs={{0,1},{1,0},{2,3},{3,2},{4,5},{5,4},{6,7},{7,6},{8,9},{9,8},{10,11... | collective-permute-start | bytes 1990664 | tf_op jit(solution)/shard_map/ppermute | solution.py:203
  109.0 6.7 %collective-permute-start.20 = (bf16[96,1536]{1,0:T(8,128)(2,1)S(1)}, bf16[96,1536]{1,0:T(8,128)(2,1)S(1)}, u32[]{:S(2)}, u32[]{:S(2)}) collective-permute-start(bf16[96,1536]{1,0:T(8,128)(2,1)S(1)} %get-tuple-element.34), channel_id=1, source_target_pairs={{0,8},{2,10},{8,16},{10,18},{16,24},{18,26},{24,28},{26,30},{28,20... | collective-permute-start | bytes 884744 | tf_op jit(solution)/shard_map/ppermute | solution.py:100
  110.6 6.7 %collective-permute-start.23 = (bf16[96,1536]{1,0:T(8,128)(2,1)S(1)}, bf16[96,1536]{1,0:T(8,128)(2,1)S(1)}, u32[]{:S(2)}, u32[]{:S(2)}) collective-permute-start(bf16[96,1536]{1,0:T(8,128)(2,1)S(1)} %get-tuple-element.35), channel_id=1, source_target_pairs={{0,4},{2,6},{8,0},{10,2},{16,8},{18,10},{24,16},{26,18},{28,24},{3... | collective-permute-start | bytes 884744 | tf_op jit(solution)/shard_map/ppermute | solution.py:100
  118.3 14.9 %collective-permute-start.21 = (bf16[96,1536]{1,0:T(8,128)(2,1)}, bf16[96,1536]{1,0:T(8,128)(2,1)}, u32[]{:S(2)}, u32[]{:S(2)}) collective-permute-start(bf16[96,1536]{1,0:T(8,128)(2,1)} %get-tuple-element.168), channel_id=1, source_target_pairs={{0,8},{2,10},{8,16},{10,18},{16,24},{18,26},{24,28},{26,30},{28,20... | collective-permute-start | bytes 884744 | tf_op jit(solution)/shard_map/ppermute | solution.py:100
  119.8 13.9 %collective-permute-start.24 = (bf16[96,1536]{1,0:T(8,128)(2,1)}, bf16[96,1536]{1,0:T(8,128)(2,1)}, u32[]{:S(2)}, u32[]{:S(2)}) collective-permute-start(bf16[96,1536]{1,0:T(8,128)(2,1)} %get-tuple-element.167), channel_id=1, source_target_pairs={{0,4},{2,6},{8,0},{10,2},{16,8},{18,10},{24,16},{26,18},{28,24},{3... | collective-permute-start | bytes 884744 | tf_op jit(solution)/shard_map/ppermute | solution.py:100
  133.1 3.3 %collective-permute-start.28 = (bf16[7,7,768]{2,1,0:T(8,128)(2,1)S(1)}, bf16[7,7,768]{2,1,0:T(8,128)(2,1)S(1)}, u32[]{:S(2)}, u32[]{:S(2)}) collective-permute-start(bf16[7,7,768]{2,1,0:T(8,128)(2,1)S(1)} %multiply_convert_fusion.3), channel_id=1, source_target_pairs={{0,2},{2,0},{4,6},{6,4},{8,10},{10,8},{12,14},{14,12},{16,18},{18,... | collective-permute-start | bytes 225800 | tf_op jit(solution)/shard_map/ppermute | solution.py:233
  133.2 5.4 %collective-permute-start.29 = (bf16[7,7,768]{2,1,0:T(8,128)(2,1)S(1)}, bf16[7,7,768]{2,1,0:T(8,128)(2,1)S(1)}, u32[]{:S(2)}, u32[]{:S(2)}) collective-permute-start(bf16[7,7,768]{2,1,0:T(8,128)(2,1)S(1)} %multiply_convert_fusion.3), channel_id=1, source_target_pairs={{0,4},{2,6},{4,0},{6,2},{8,12},{10,14},{12,8},{14,10},{16,20},{18,... | collective-permute-start | bytes 225800 | tf_op jit(solution)/shard_map/ppermute | solution.py:233
  133.7 5.7 %collective-permute-start.30 = (bf16[7,7,768]{2,1,0:T(8,128)(2,1)S(1)}, bf16[7,7,768]{2,1,0:T(8,128)(2,1)S(1)}, u32[]{:S(2)}, u32[]{:S(2)}) collective-permute-start(bf16[7,7,768]{2,1,0:T(8,128)(2,1)S(1)} %multiply_convert_fusion.3), channel_id=1, source_target_pairs={{0,6},{2,4},{4,2},{6,0},{8,14},{10,12},{12,10},{14,8},{16,22},{18,... | collective-permute-start | bytes 225800 | tf_op jit(solution)/shard_map/ppermute | solution.py:233
  136.4 20.6 %collective-permute-start.22 = (bf16[96,1536]{1,0:T(8,128)(2,1)S(1)}, bf16[96,1536]{1,0:T(8,128)(2,1)S(1)}, u32[]{:S(2)}, u32[]{:S(2)}) collective-permute-start(bf16[96,1536]{1,0:T(8,128)(2,1)S(1)} %get-tuple-element.166), channel_id=1, source_target_pairs={{0,8},{2,10},{8,16},{10,18},{16,24},{18,26},{24,28},{26,30},{28,20... | collective-permute-start | bytes 884744 | tf_op jit(solution)/shard_map/ppermute | solution.py:100
  138.6 19.7 %collective-permute-start.25 = (bf16[96,1536]{1,0:T(8,128)(2,1)S(1)}, bf16[96,1536]{1,0:T(8,128)(2,1)S(1)}, u32[]{:S(2)}, u32[]{:S(2)}) collective-permute-start(bf16[96,1536]{1,0:T(8,128)(2,1)S(1)} %get-tuple-element.165), channel_id=1, source_target_pairs={{0,4},{2,6},{8,0},{10,2},{16,8},{18,10},{24,16},{26,18},{28,24},{3... | collective-permute-start | bytes 884744 | tf_op jit(solution)/shard_map/ppermute | solution.py:100
  139.5 10.3 %collective-permute-start.35 = (bf16[7,7,768]{2,1,0:T(8,128)(2,1)S(1)}, bf16[7,7,768]{2,1,0:T(8,128)(2,1)S(1)}, u32[]{:S(2)}, u32[]{:S(2)}) collective-permute-start(bf16[7,7,768]{2,1,0:T(8,128)(2,1)S(1)} %add_convert_fusion.29), channel_id=1, source_target_pairs={{0,8},{2,10},{4,12},{6,14},{8,0},{10,2},{12,4},{14,6},{16,24},{18,... | collective-permute-start | bytes 225800 | tf_op jit(solution)/shard_map/ppermute | solution.py:233
  141.2 13.0 %collective-permute-start.36 = (bf16[7,7,768]{2,1,0:T(8,128)(2,1)S(1)}, bf16[7,7,768]{2,1,0:T(8,128)(2,1)S(1)}, u32[]{:S(2)}, u32[]{:S(2)}) collective-permute-start(bf16[7,7,768]{2,1,0:T(8,128)(2,1)S(1)} %add_convert_fusion.29), channel_id=1, source_target_pairs={{0,16},{2,18},{4,20},{6,22},{8,24},{10,26},{12,28},{14,30},{16,0},... | collective-permute-start | bytes 225800 | tf_op jit(solution)/shard_map/ppermute | solution.py:233
  142.6 12.9 %collective-permute-start.37 = (bf16[7,7,768]{2,1,0:T(8,128)(2,1)S(1)}, bf16[7,7,768]{2,1,0:T(8,128)(2,1)S(1)}, u32[]{:S(2)}, u32[]{:S(2)}) collective-permute-start(bf16[7,7,768]{2,1,0:T(8,128)(2,1)S(1)} %add_convert_fusion.29), channel_id=1, source_target_pairs={{0,24},{2,26},{4,28},{6,30},{8,16},{10,18},{12,20},{14,22},{16,8},... | collective-permute-start | bytes 225800 | tf_op jit(solution)/shard_map/ppermute | solution.py:233
  149.8 42.2 %collective-permute-start.8 = (bf16[3,144,768]{2,1,0:T(8,128)(2,1)S(1)}, bf16[3,144,768]{2,1,0:T(8,128)(2,1)S(1)}, u32[]{:S(2)}, u32[]{:S(2)}) collective-permute-start(bf16[3,144,768]{2,1,0:T(8,128)(2,1)S(1)} %bitcast.33), channel_id=1, source_target_pairs={{0,2},{2,4},{4,6},{6,8},{8,10},{10,12},{12,14},{14,16},{16,18},{18... | collective-permute-start | bytes 1990664 | tf_op jit(solution)/shard_map/ppermute | solution.py:14
  154.2 38.2 %collective-permute-start.9 = (bf16[3,144,768]{2,1,0:T(8,128)(2,1)S(1)}, bf16[3,144,768]{2,1,0:T(8,128)(2,1)S(1)}, u32[]{:S(2)}, u32[]{:S(2)}) collective-permute-start(bf16[3,144,768]{2,1,0:T(8,128)(2,1)S(1)} %bitcast.34), channel_id=1, source_target_pairs={{2,0},{4,2},{6,4},{8,6},{10,8},{12,10},{14,12},{16,14},{18,16},{20... | collective-permute-start | bytes 1990664 | tf_op jit(solution)/shard_map/ppermute | solution.py:15
  155.5 17.9 %collective-permute-start.16 = (bf16[96,1536]{1,0:T(8,128)(2,1)S(1)}, bf16[96,1536]{1,0:T(8,128)(2,1)S(1)}, u32[]{:S(2)}, u32[]{:S(2)}) collective-permute-start(bf16[96,1536]{1,0:T(8,128)(2,1)S(1)} %get-tuple-element.32), channel_id=1, source_target_pairs={{0,8},{2,10},{8,16},{10,18},{16,24},{18,26},{24,28},{26,30},{28,20... | collective-permute-start | bytes 884744 | tf_op jit(solution)/shard_map/ppermute | solution.py:100
  157.0 17.3 %collective-permute-start.17 = (bf16[96,1536]{1,0:T(8,128)(2,1)S(1)}, bf16[96,1536]{1,0:T(8,128)(2,1)S(1)}, u32[]{:S(2)}, u32[]{:S(2)}) collective-permute-start(bf16[96,1536]{1,0:T(8,128)(2,1)S(1)} %get-tuple-element.33), channel_id=1, source_target_pairs={{0,4},{2,6},{8,0},{10,2},{16,8},{18,10},{24,16},{26,18},{28,24},{3... | collective-permute-start | bytes 884744 | tf_op jit(solution)/shard_map/ppermute | solution.py:100
  159.5 20.3 %collective-permute-start.26 = (bf16[96,1536]{1,0:T(8,128)(2,1)S(1)}, bf16[96,1536]{1,0:T(8,128)(2,1)S(1)}, u32[]{:S(2)}, u32[]{:S(2)}) collective-permute-start(bf16[96,1536]{1,0:T(8,128)(2,1)S(1)} %get-tuple-element.164), channel_id=1, source_target_pairs={{0,8},{2,10},{8,16},{10,18},{16,24},{18,26},{24,28},{26,30},{28,20... | collective-permute-start | bytes 884744 | tf_op jit(solution)/shard_map/ppermute | solution.py:100
  173.4 9.6 %collective-permute-start.27 = (bf16[96,1536]{1,0:T(8,128)(2,1)S(1)}, bf16[96,1536]{1,0:T(8,128)(2,1)S(1)}, u32[]{:S(2)}, u32[]{:S(2)}) collective-permute-start(bf16[96,1536]{1,0:T(8,128)(2,1)S(1)} %get-tuple-element.163), channel_id=1, source_target_pairs={{0,4},{2,6},{8,0},{10,2},{16,8},{18,10},{24,16},{26,18},{28,24},{3... | collective-permute-start | bytes 884744 | tf_op jit(solution)/shard_map/ppermute | solution.py:100
  175.5 9.6 %collective-permute-start.39 = (bf16[96,1536]{1,0:T(8,128)(2,1)S(1)}, bf16[96,1536]{1,0:T(8,128)(2,1)S(1)}, u32[]{:S(2)}, u32[]{:S(2)}) collective-permute-start(bf16[96,1536]{1,0:T(8,128)(2,1)S(1)} %get-tuple-element.44), channel_id=1, source_target_pairs={{0,8},{2,10},{8,16},{10,18},{16,24},{18,26},{24,28},{26,30},{28,20... | collective-permute-start | bytes 884744 | tf_op jit(solution)/shard_map/ppermute | solution.py:100
  179.8 9.3 %collective-permute-start.42 = (bf16[96,1536]{1,0:T(8,128)(2,1)S(1)}, bf16[96,1536]{1,0:T(8,128)(2,1)S(1)}, u32[]{:S(2)}, u32[]{:S(2)}) collective-permute-start(bf16[96,1536]{1,0:T(8,128)(2,1)S(1)} %get-tuple-element.45), channel_id=1, source_target_pairs={{0,4},{2,6},{8,0},{10,2},{16,8},{18,10},{24,16},{26,18},{28,24},{3... | collective-permute-start | bytes 884744 | tf_op jit(solution)/shard_map/ppermute | solution.py:100
  184.2 9.7 %collective-permute-start.31 = (bf16[96,1536]{1,0:T(8,128)(2,1)S(1)}, bf16[96,1536]{1,0:T(8,128)(2,1)S(1)}, u32[]{:S(2)}, u32[]{:S(2)}) collective-permute-start(bf16[96,1536]{1,0:T(8,128)(2,1)S(1)} %get-tuple-element.38), channel_id=1, source_target_pairs={{0,8},{2,10},{8,16},{10,18},{16,24},{18,26},{24,28},{26,30},{28,20... | collective-permute-start | bytes 884744 | tf_op jit(solution)/shard_map/ppermute | solution.py:100
  185.1 10.4 %collective-permute-start.32 = (bf16[96,1536]{1,0:T(8,128)(2,1)S(1)}, bf16[96,1536]{1,0:T(8,128)(2,1)S(1)}, u32[]{:S(2)}, u32[]{:S(2)}) collective-permute-start(bf16[96,1536]{1,0:T(8,128)(2,1)S(1)} %get-tuple-element.39), channel_id=1, source_target_pairs={{0,4},{2,6},{8,0},{10,2},{16,8},{18,10},{24,16},{26,18},{28,24},{3... | collective-permute-start | bytes 884744 | tf_op jit(solution)/shard_map/ppermute | solution.py:100
  190.3 7.0 %collective-permute-start.40 = (bf16[96,1536]{1,0:T(8,128)(2,1)S(1)}, bf16[96,1536]{1,0:T(8,128)(2,1)S(1)}, u32[]{:S(2)}, u32[]{:S(2)}) collective-permute-start(bf16[96,1536]{1,0:T(8,128)(2,1)S(1)} %get-tuple-element.156), channel_id=1, source_target_pairs={{0,8},{2,10},{8,16},{10,18},{16,24},{18,26},{24,28},{26,30},{28,20... | collective-permute-start | bytes 884744 | tf_op jit(solution)/shard_map/ppermute | solution.py:100
  192.0 7.1 %collective-permute-start.43 = (bf16[96,1536]{1,0:T(8,128)(2,1)S(1)}, bf16[96,1536]{1,0:T(8,128)(2,1)S(1)}, u32[]{:S(2)}, u32[]{:S(2)}) collective-permute-start(bf16[96,1536]{1,0:T(8,128)(2,1)S(1)} %get-tuple-element.155), channel_id=1, source_target_pairs={{0,4},{2,6},{8,0},{10,2},{16,8},{18,10},{24,16},{26,18},{28,24},{3... | collective-permute-start | bytes 884744 | tf_op jit(solution)/shard_map/ppermute | solution.py:100
  200.7 15.0 %collective-permute-start.41 = (bf16[96,1536]{1,0:T(8,128)(2,1)S(1)}, bf16[96,1536]{1,0:T(8,128)(2,1)S(1)}, u32[]{:S(2)}, u32[]{:S(2)}) collective-permute-start(bf16[96,1536]{1,0:T(8,128)(2,1)S(1)} %get-tuple-element.154), channel_id=1, source_target_pairs={{0,8},{2,10},{8,16},{10,18},{16,24},{18,26},{24,28},{26,30},{28,20... | collective-permute-start | bytes 884744 | tf_op jit(solution)/shard_map/ppermute | solution.py:100
  202.5 13.2 %collective-permute-start.44 = (bf16[96,1536]{1,0:T(8,128)(2,1)S(1)}, bf16[96,1536]{1,0:T(8,128)(2,1)S(1)}, u32[]{:S(2)}, u32[]{:S(2)}) collective-permute-start(bf16[96,1536]{1,0:T(8,128)(2,1)S(1)} %get-tuple-element.153), channel_id=1, source_target_pairs={{0,4},{2,6},{8,0},{10,2},{16,8},{18,10},{24,16},{26,18},{28,24},{3... | collective-permute-start | bytes 884744 | tf_op jit(solution)/shard_map/ppermute | solution.py:100
  213.6 6.7 %collective-permute-start.33 = (bf16[96,1536]{1,0:T(8,128)(2,1)S(1)}, bf16[96,1536]{1,0:T(8,128)(2,1)S(1)}, u32[]{:S(2)}, u32[]{:S(2)}) collective-permute-start(bf16[96,1536]{1,0:T(8,128)(2,1)S(1)} %get-tuple-element.40), channel_id=1, source_target_pairs={{0,8},{2,10},{8,16},{10,18},{16,24},{18,26},{24,28},{26,30},{28,20... | collective-permute-start | bytes 884744 | tf_op jit(solution)/shard_map/ppermute | solution.py:100
  215.4 6.7 %collective-permute-start.34 = (bf16[96,1536]{1,0:T(8,128)(2,1)S(1)}, bf16[96,1536]{1,0:T(8,128)(2,1)S(1)}, u32[]{:S(2)}, u32[]{:S(2)}) collective-permute-start(bf16[96,1536]{1,0:T(8,128)(2,1)S(1)} %get-tuple-element.41), channel_id=1, source_target_pairs={{0,4},{2,6},{8,0},{10,2},{16,8},{18,10},{24,16},{26,18},{28,24},{3... | collective-permute-start | bytes 884744 | tf_op jit(solution)/shard_map/ppermute | solution.py:100
  216.9 6.6 %collective-permute-start.45 = (bf16[96,1536]{1,0:T(8,128)(2,1)S(1)}, bf16[96,1536]{1,0:T(8,128)(2,1)S(1)}, u32[]{:S(2)}, u32[]{:S(2)}) collective-permute-start(bf16[96,1536]{1,0:T(8,128)(2,1)S(1)} %get-tuple-element.150), channel_id=1, source_target_pairs={{0,2},{2,0},{4,6},{6,4},{8,10},{10,8},{12,14},{14,12},{16,18},{18,... | collective-permute-start | bytes 884744 | tf_op jit(solution)/shard_map/ppermute | solution.py:110
  223.4 1.6 collective-permute-start.38
  (65 other events, 468.4 us)

commit v2 on v0

--- a/solution.py
+++ b/solution.py
@@ -226,7 +226,7 @@
                 sums[which] = tie(sums[which], sent)
             if step == 3 and which == 0:
                 sums[which] = tie(sums[which], grad_conv)
-            if step == 4 and which == 0:
+            if step == 3 and which == 1:
                 kernel_sum = terms(tie(grad_conv, early), range(7))
                 sums[which] = tie(sums[which], kernel_sum)
             if step == last and which == 1:
@@ -234,7 +234,7 @@
                     cot_own + conv_back(tie(grad_pad, middle), kernel, height, width)
                 ).astype(jnp.bfloat16)
                 sums[which] = tie(sums[which], grad_feature)
-            if step > 4 and span < rows:
+            if step > 3 and which == 1 and span < rows:
                 other = lax.ppermute(kernel_sum, "rows", [(i, i ^ span) for i in range(rows)])
                 total = kernel_sum.astype(jnp.float32) + other.astype(jnp.float32)
                 span *= 2

time: 218 us -> 233 us (1.069)
  waiting for transfers between devices: 51.2 us -> 67.6 us
    ppermute x28, waiting for transfers between devices: 24.1 us -> 50.1 us  [ring_step(): got = lax.ppermute(sums[side], 'rows', ring_pairs(chips, way))]
    ppermute x4, waiting for transfers between devices: 20.5 us -> 6.95 us  [shards(): lax.ppermute(kernel_sum, 'rows', [(i, i ^ span) for i in range(rows)])]
    ppermute x1, waiting for transfers between devices: 3.34 us -> 6.47 us  [shards(): got = lax.ppermute(sent[0], 'chan', cross).astype(jnp.float32)]
    ppermute x4, starting transfers between devices: 1.49 us -> 4.23 us  [shards(): lax.ppermute(kernel_sum, 'rows', [(i, i ^ span) for i in range(rows)])]
    convert_element_type x12 -> x11, other arithmetic: 12 us -> 10.2 us  [ring_step(): result.append(total.astype(jnp.bfloat16))]
  transfers between devices with their start and end apart: 44 -> 44, of which waited for: 17 -> 24; matrix products, arithmetic and copies ran while one was open for 34% -> 25% of each run, Pallas kernels for 0% -> 0%
where the time goes in v2:
time: 233 us
  starting transfers between devices  67.9 us (29%)
  waiting for transfers between devices  67.6 us (29%)
  other arithmetic  53.2 us (23%)
  matrix products  37.8 us (16%)
  local copies, waits for them, and re-layouts  4.11 us (2%)
  between operations  2.44 us (1%)
    ppermute x28, waiting for transfers between devices, ring_step(): got = lax.ppermute(sums[side], 'rows', ring_pairs(chips, way))  50.1 us
    ppermute x28, starting transfers between devices, ring_step(): got = lax.ppermute(sums[side], 'rows', ring_pairs(chips, way))  38.8 us
    dot_general x2, matrix products, pixel_sum(): lax.dot_general(left, right, (((0,), (0,)), ((), ())), preferred_element_...  14.7 us
    convert_element_type x1, other arithmetic, shards(): grad_feature = (cot_own + conv_back(tie(grad_pad, middle), kernel, height...  10.7 us
    dot_general x1, matrix products, shards(): hidden = jnp.dot(normed_both, in_part, preferred_element_type=jnp.float32)  10.2 us
    convert_element_type x11, other arithmetic, ring_step(): result.append(total.astype(jnp.bfloat16))  10.2 us
    convert_element_type x1, other arithmetic, shards(): conv_local = conv_taps(padded, kernel, height, width).astype(jnp.bfloat16)  9.73 us
    ppermute x1, starting transfers between devices, shards(): lax.ppermute(normed, 'rows', swap)  9.54 us
  transfers between devices with their start and end apart: 44, of which 24 were waited for; matrix products, arithmetic and copies ran while one was open for 25% of the time, Pallas kernels for 0%

profile of v2, /device:TPU:0, one launch (start us, length us, event | category | flops | bytes accessed | tf_op | source)
XLA Modules:
  0.0 233.0 jit_solution(7063278386996923810)
XLA Ops:
  0.6 1.4 collective-permute-start.1
  2.1 3.1 %collective-permute-start = (bf16[3,144,768]{2,1,0:T(8,128)(2,1)}, bf16[3,144,768]{2,1,0:T(8,128)(2,1)S(1)}, u32[]{:S(2)}, u32[]{:S(2)}) collective-permute-start(bf16[3,144,768]{2,1,0:T(8,128)(2,1)} %param.7), channel_id=1, source_target_pairs={{0,2},{2,4},{4,6},{6,8},{8,10},{10,12},{12,14},{14,16},{16,18},{18... | collective-permute-start | bytes 1990664 | tf_op jit(solution)/shard_map/ppermute | solution.py:14
  5.2 2.7 %fusion.28 = bf16[432,1536]{1,0:T(8,128)(2,1)} fusion(bf16[3,144,1536]{2,1,0:T(8,128)(2,1)} %param.13, f32[1536]{0:T(1024)} %param.10), kind=kLoop, calls=%fused_computation.87 | loop fusion | flops 1990656 | bytes 2660352 | tf_op jit(solution)/shard_map/convert_element_type | solution.py:131
  7.8 2.5 %collective-permute-start.3 = (bf16[432,1536]{1,0:T(8,128)(2,1)}, bf16[432,1536]{1,0:T(8,128)(2,1)}, u32[]{:S(2)}, u32[]{:S(2)}) collective-permute-start(bf16[432,1536]{1,0:T(8,128)(2,1)} %fusion.28), channel_id=1, source_target_pairs={{0,2},{2,0},{4,6},{6,4},{8,10},{10,8},{12,14},{14,12},{16,18},{18,... | collective-permute-start | bytes 3981320 | tf_op jit(solution)/shard_map/ppermute | solution.py:134
  11.8 2.0 fusion.37
  15.2 9.7 %fusion.136 = bf16[3,144,768]{2,1,0:T(8,128)(2,1)S(1)} fusion(bf16[3,144,768]{2,1,0:T(8,128)(2,1)S(1)} %collective-permute-done.1, bf16[3,144,768]{2,1,0:T(8,128)(2,1)S(1)} %copy-done, bf16[3,144,768]{2,1,0:T(8,128)(2,1)S(1)} %copy-done.5, f32[768]{0:T(1024)S(1)} %get-tuple-element.142, f32[768]{0:T(1024)S(1)} %get-tuple-element.143, ...), kind=kLoop, calls=%fused_computation.252 | loop fusion | flops 48771072 | bytes 33328128 | tf_op jit(solution)/shard_map/convert_element_type | solution.py:142
  24.9 1.6 collective-permute-start.2
  26.5 7.9 %fusion.9 = f32[864,1536]{1,0:T(8,128)} fusion(bf16[3072,1536]{1,0:T(8,128)(2,1)S(1)} %bitcast.44, s32[]{:T(128)S(6)} %select_n.194, bf16[432,1536]{1,0:T(8,128)(2,1)} %collective-permute-done.3, bf16[432,1536]{1,0:T(8,128)(2,1)} %fusion.28), kind=kOutput, calls=%fused_computation.65 | convolution fusion | flops 4082171904 | bytes 12681220 | tf_op jit(solution)/shard_map/dot_general | solution.py:137
  36.6 1.6 fusion.25
  38.2 9.5 %collective-permute-start.4 = (bf16[432,1536]{1,0:T(8,128)(2,1)}, bf16[432,1536]{1,0:T(8,128)(2,1)}, u32[]{:S(2)}, u32[]{:S(2)}) collective-permute-start(bf16[432,1536]{1,0:T(8,128)(2,1)} %fusion.25), channel_id=1, source_target_pairs={{0,2},{2,0},{4,6},{6,4},{8,10},{10,8},{12,14},{14,12},{16,18},{18,... | collective-permute-start | bytes 3981320 | tf_op jit(solution)/shard_map/ppermute | solution.py:163
  48.4 2.4 %collective-permute-done.4 = bf16[432,1536]{1,0:T(8,128)(2,1)} collective-permute-done((bf16[432,1536]{1,0:T(8,128)(2,1)}, bf16[432,1536]{1,0:T(8,128)(2,1)}, u32[]{:S(2)}, u32[]{:S(2)}) %collective-permute-start.4) | collective-permute-done | bytes 1327136 | tf_op jit(solution)/shard_map/ppermute | solution.py:163
  50.8 10.2 %fusion.8 = (bf16[864,1536]{1,0:T(8,128)(2,1)S(1)}, f32[864,1536]{1,0:T(8,128)S(1)}) fusion(f32[864,1536]{1,0:T(8,128)} %fusion.9, bf16[1536,3072]{1,0:T(8,128)(2,1)} %param.11, s32[]{:T(128)S(6)} %select_n.194, bf16[432,1536]{1,0:T(8,128)(2,1)} %collective-permute-done.4, bf16[432,1536]{1,0:T(8,128)(2,1)} %fusion.25), kind=kOutput, calls=%fused_computation.63 | convolution fusion | flops 4108713984 | bytes 20643844 | tf_op jit(solution)/shard_map/dot_general | solution.py:164
  61.0 7.4 %fusion.1 = bf16[1536,1536]{1,0:T(8,128)(2,1)S(1)} fusion(f32[864,1536]{1,0:T(8,128)S(1)} %get-tuple-element.189, bf16[432,1536]{1,0:T(8,128)(2,1)} %collective-permute-done.3, bf16[432,1536]{1,0:T(8,128)(2,1)} %fusion.28), kind=kOutput, calls=%fused_computation.54 | convolution fusion | flops 4098834432 | bytes 12681216 | tf_op jit(solution)/shard_map/dot_general | solution.py:169
  68.5 4.0 %collective-permute-start.13 = (bf16[96,1536]{1,0:T(8,128)(2,1)S(1)}, bf16[96,1536]{1,0:T(8,128)(2,1)S(1)}, u32[]{:S(2)}, u32[]{:S(2)}) collective-permute-start(bf16[96,1536]{1,0:T(8,128)(2,1)S(1)} %get-tuple-element.176), channel_id=1, source_target_pairs={{0,4},{2,6},{8,0},{10,2},{16,8},{18,10},{24,16},{26,18},{28,24},{3... | collective-permute-start | bytes 884744 | tf_op jit(solution)/shard_map/ppermute | solution.py:95
  72.5 2.4 %collective-permute-start.10 = (bf16[96,1536]{1,0:T(8,128)(2,1)S(1)}, bf16[96,1536]{1,0:T(8,128)(2,1)S(1)}, u32[]{:S(2)}, u32[]{:S(2)}) collective-permute-start(bf16[96,1536]{1,0:T(8,128)(2,1)S(1)} %get-tuple-element.177), channel_id=1, source_target_pairs={{0,8},{2,10},{8,16},{10,18},{16,24},{18,26},{24,28},{26,30},{28,20... | collective-permute-start | bytes 884744 | tf_op jit(solution)/shard_map/ppermute | solution.py:95
  75.0 7.3 %fusion = bf16[1536,1536]{1,0:T(8,128)(2,1)S(1)} fusion(bf16[864,1536]{1,0:T(8,128)(2,1)S(1)} %get-tuple-element.188, bf16[432,1536]{1,0:T(8,128)(2,1)} %collective-permute-done.4, bf16[432,1536]{1,0:T(8,128)(2,1)} %fusion.25), kind=kOutput, calls=%fused_computation.53 | convolution fusion | flops 4086890496 | bytes 10027008 | tf_op jit(solution)/shard_map/dot_general | solution.py:169
  82.5 2.0 collective-permute-start.18
  84.5 2.3 fusion.22
  87.2 2.0 collective-permute-start.11
  89.1 3.2 %collective-permute-done.19 = bf16[96,1536]{1,0:T(8,128)(2,1)S(1)} collective-permute-done((bf16[96,1536]{1,0:T(8,128)(2,1)S(1)}, bf16[96,1536]{1,0:T(8,128)(2,1)S(1)}, u32[]{:S(2)}, u32[]{:S(2)}) %collective-permute-start.19) | collective-permute-done | bytes 294944 | tf_op jit(solution)/shard_map/ppermute | solution.py:95
  92.6 5.2 %collective-permute-done.14 = bf16[96,1536]{1,0:T(8,128)(2,1)S(1)} collective-permute-done((bf16[96,1536]{1,0:T(8,128)(2,1)S(1)}, bf16[96,1536]{1,0:T(8,128)(2,1)S(1)}, u32[]{:S(2)}, u32[]{:S(2)}) %collective-permute-start.14) | collective-permute-done | bytes 294944 | tf_op jit(solution)/shard_map/ppermute | solution.py:95
  98.8 2.8 %multiply_reduce_fusion = (f32[432]{0:T(512)S(1)}, f32[432]{0:T(512)S(1)}, f32[432,1536]{1,0:T(8,128)S(1)}) fusion(f32[1536]{0:T(1024)S(1)} %copy-done.61, f32[432]{0:T(512)S(1)} %copy-done.63, f32[432]{0:T(512)S(1)} %broadcast_multiply_fusion, bf16[432,768]{1,0:T(8,128)(2,1)S(1)} %get-tuple-element.179, bf16[432,768]{1,0:T(8,128)(2,1)S(1)} %get-tuple-element.178, ...), kind=kOutput, calls=%fused_computation.93 | convolution fusion | flops 2046393600 | bytes 11369860 | tf_op jit(solution)/shard_map/dot_general | solution.py:175
  101.7 1.6 collective-permute-start.7
  103.9 1.7 collective-permute-start.20
  106.0 5.5 %collective-permute-done.20 = bf16[96,1536]{1,0:T(8,128)(2,1)S(1)} collective-permute-done((bf16[96,1536]{1,0:T(8,128)(2,1)S(1)}, bf16[96,1536]{1,0:T(8,128)(2,1)S(1)}, u32[]{:S(2)}, u32[]{:S(2)}) %collective-permute-start.20) | collective-permute-done | bytes 294944 | tf_op jit(solution)/shard_map/ppermute | solution.py:95
  112.7 6.5 %collective-permute-done.6 = bf16[432,768]{1,0:T(8,128)(2,1)S(1)} collective-permute-done((bf16[432,768]{1,0:T(8,128)(2,1)S(1)}, bf16[432,768]{1,0:T(8,128)(2,1)S(1)}, u32[]{:S(2)}, u32[]{:S(2)}) %collective-permute-start.6) | collective-permute-done | bytes 663584 | tf_op jit(solution)/shard_map/ppermute | solution.py:192
  119.7 3.2 %fusion.133 = (f32[768]{0:T(1024)S(1)}, f32[768]{0:T(1024)S(1)}, f32[768]{0:T(1024)S(1)}, f32[768]{0:T(1024)S(1)}, f32[768]{0:T(1024)S(1)}, /*index=5*/f32[768]{...) fusion(bf16[3,144,768]{2,1,0:T(8,128)(2,1)S(1)} %bitcast.30, ...), kind=kLoop, calls=%fused_computation.245 | loop fusion | flops 18233856 | bytes 12662784 | tf_op jit(solution)/shard_map/reduce_sum | solution.py:50
  123.0 3.3 %fusion.134 = (f32[768]{0:T(1024)S(1)}, f32[768]{0:T(1024)S(1)}, f32[768]{0:T(1024)S(1)}, f32[768]{0:T(1024)S(1)}, f32[768]{0:T(1024)S(1)}, /*index=5*/f32[768]{...) fusion(bf16[3,144,768]{2,1,0:T(8,128)(2,1)S(1)} %bitcast.31, ...), kind=kLoop, calls=%fused_computation.246 | loop fusion | flops 18233856 | bytes 12662784 | tf_op jit(solution)/shard_map/reduce_sum | solution.py:50
  126.4 2.1 fusion.132
  130.2 1.5 collective-permute-start.21
  134.6 4.8 %collective-permute-done.23 = bf16[96,1536]{1,0:T(8,128)(2,1)S(1)} collective-permute-done((bf16[96,1536]{1,0:T(8,128)(2,1)S(1)}, bf16[96,1536]{1,0:T(8,128)(2,1)S(1)}, u32[]{:S(2)}, u32[]{:S(2)}) %collective-permute-start.23) | collective-permute-done | bytes 294944 | tf_op jit(solution)/shard_map/ppermute | solution.py:95
  143.6 4.8 %collective-permute-done.29 = bf16[7,7,768]{2,1,0:T(8,128)(2,1)S(1)} collective-permute-done((bf16[7,7,768]{2,1,0:T(8,128)(2,1)S(1)}, bf16[7,7,768]{2,1,0:T(8,128)(2,1)S(1)}, u32[]{:S(2)}, u32[]{:S(2)}) %collective-permute-start.29) | collective-permute-done | bytes 75296 | tf_op jit(solution)/shard_map/ppermute | solution.py:238
  151.0 3.1 %collective-permute-start.8 = (bf16[3,144,768]{2,1,0:T(8,128)(2,1)S(1)}, bf16[3,144,768]{2,1,0:T(8,128)(2,1)S(1)}, u32[]{:S(2)}, u32[]{:S(2)}) collective-permute-start(bf16[3,144,768]{2,1,0:T(8,128)(2,1)S(1)} %bitcast.34), channel_id=1, source_target_pairs={{0,2},{2,4},{4,6},{6,8},{8,10},{10,12},{12,14},{14,16},{16,18},{18... | collective-permute-start | bytes 1990664 | tf_op jit(solution)/shard_map/ppermute | solution.py:14
  154.1 2.0 collective-permute-start.16
  156.3 3.2 %collective-permute-start.43 = (bf16[7,7,768]{2,1,0:T(8,128)(2,1)S(1)}, bf16[7,7,768]{2,1,0:T(8,128)(2,1)S(1)}, u32[]{:S(2)}, u32[]{:S(2)}) collective-permute-start(bf16[7,7,768]{2,1,0:T(8,128)(2,1)S(1)} %add_convert_fusion.29), channel_id=1, source_target_pairs={{0,16},{2,18},{4,20},{6,22},{8,24},{10,26},{12,28},{14,30},{16,0},... | collective-permute-start | bytes 225800 | tf_op jit(solution)/shard_map/ppermute | solution.py:249
  160.7 7.5 %collective-permute-done.16 = bf16[96,1536]{1,0:T(8,128)(2,1)S(1)} collective-permute-done((bf16[96,1536]{1,0:T(8,128)(2,1)S(1)}, bf16[96,1536]{1,0:T(8,128)(2,1)S(1)}, u32[]{:S(2)}, u32[]{:S(2)}) %collective-permute-start.16) | collective-permute-done | bytes 294944 | tf_op jit(solution)/shard_map/ppermute | solution.py:95
  171.4 2.2 collective-permute-done.43
  174.9 2.0 collective-permute-start.36
  179.1 4.8 %collective-permute-start.30 = (bf16[96,1536]{1,0:T(8,128)(2,1)S(1)}, bf16[96,1536]{1,0:T(8,128)(2,1)S(1)}, u32[]{:S(2)}, u32[]{:S(2)}) collective-permute-start(bf16[96,1536]{1,0:T(8,128)(2,1)S(1)} %get-tuple-element.34), channel_id=1, source_target_pairs={{0,8},{2,10},{8,16},{10,18},{16,24},{18,26},{24,28},{26,30},{28,20... | collective-permute-start | bytes 884744 | tf_op jit(solution)/shard_map/ppermute | solution.py:95
  185.2 3.9 %collective-permute-start.40 = (bf16[96,1536]{1,0:T(8,128)(2,1)S(1)}, bf16[96,1536]{1,0:T(8,128)(2,1)S(1)}, u32[]{:S(2)}, u32[]{:S(2)}) collective-permute-start(bf16[96,1536]{1,0:T(8,128)(2,1)S(1)} %get-tuple-element.152), channel_id=1, source_target_pairs={{0,4},{2,6},{8,0},{10,2},{16,8},{18,10},{24,16},{26,18},{28,24},{3... | collective-permute-start | bytes 884744 | tf_op jit(solution)/shard_map/ppermute | solution.py:95
  191.3 3.4 %collective-permute-done.31 = bf16[96,1536]{1,0:T(8,128)(2,1)S(1)} collective-permute-done((bf16[96,1536]{1,0:T(8,128)(2,1)S(1)}, bf16[96,1536]{1,0:T(8,128)(2,1)S(1)}, u32[]{:S(2)}, u32[]{:S(2)}) %collective-permute-start.31) | collective-permute-done | bytes 294944 | tf_op jit(solution)/shard_map/ppermute | solution.py:95
  194.7 6.3 %collective-permute-done.40 = bf16[96,1536]{1,0:T(8,128)(2,1)S(1)} collective-permute-done((bf16[96,1536]{1,0:T(8,128)(2,1)S(1)}, bf16[96,1536]{1,0:T(8,128)(2,1)S(1)}, u32[]{:S(2)}, u32[]{:S(2)}) %collective-permute-start.40) | collective-permute-done | bytes 294944 | tf_op jit(solution)/shard_map/ppermute | solution.py:95
  202.1 1.5 add_convert_fusion.2
  203.6 2.1 collective-permute-start.41
  206.2 10.7 %add_convert_fusion = bf16[3,144,768]{2,1,0:T(8,128)(2,1)} fusion(bf16[9,150,768]{2,1,0:T(8,128)(2,1)S(1)} %select_maximum_fusion, f32[768]{0:T(1024)S(1)} %get-tuple-element.142, f32[768]{0:T(1024)S(1)} %get-tuple-element.143, f32[768]{0:T(1024)S(1)} %get-tuple-element.96, f32[768]{0:T(1024)S(1)} %get-tuple-element.97, f32[768]{0:T(1024)S(1)} %get-tuple-element.98, ...), kind=kLoop, calls=%fused_computation.249 | loop fusion | flops 49434624 | bytes 33991684 | tf_op jit(solution)/shard_map/convert_element_type | solution.py:235
  216.9 2.0 collective-permute-start.33
  220.3 5.4 %collective-permute-done.33 = bf16[96,1536]{1,0:T(8,128)(2,1)S(1)} collective-permute-done((bf16[96,1536]{1,0:T(8,128)(2,1)S(1)}, bf16[96,1536]{1,0:T(8,128)(2,1)S(1)}, u32[]{:S(2)}, u32[]{:S(2)}) %collective-permute-start.33) | collective-permute-done | bytes 294944 | tf_op jit(solution)/shard_map/ppermute | solution.py:95
  225.7 3.2 %collective-permute-done.34 = bf16[96,1536]{1,0:T(8,128)(2,1)S(1)} collective-permute-done((bf16[96,1536]{1,0:T(8,128)(2,1)S(1)}, bf16[96,1536]{1,0:T(8,128)(2,1)S(1)}, u32[]{:S(2)}, u32[]{:S(2)}) %collective-permute-start.34) | collective-permute-done | bytes 294944 | tf_op jit(solution)/shard_map/ppermute | solution.py:95
  (304 shorter events, 39.3 us)
Async XLA Ops:
  0.6 11.2 %collective-permute-start.1 = (bf16[3,144,768]{2,1,0:T(8,128)(2,1)}, bf16[3,144,768]{2,1,0:T(8,128)(2,1)S(1)}, u32[]{:S(2)}, u32[]{:S(2)}) collective-permute-start(bf16[3,144,768]{2,1,0:T(8,128)(2,1)} %param.7), channel_id=1, source_target_pairs={{2,0},{4,2},{6,4},{8,6},{10,8},{12,10},{14,12},{16,14},{18,16},{20... | collective-permute-start | bytes 1990664 | tf_op jit(solution)/shard_map/ppermute | solution.py:15
  2.1 8.9 %collective-permute-start = (bf16[3,144,768]{2,1,0:T(8,128)(2,1)}, bf16[3,144,768]{2,1,0:T(8,128)(2,1)S(1)}, u32[]{:S(2)}, u32[]{:S(2)}) collective-permute-start(bf16[3,144,768]{2,1,0:T(8,128)(2,1)} %param.7), channel_id=1, source_target_pairs={{0,2},{2,4},{4,6},{6,8},{8,10},{10,12},{12,14},{14,16},{16,18},{18... | collective-permute-start | bytes 1990664 | tf_op jit(solution)/shard_map/ppermute | solution.py:14
  7.8 18.7 %collective-permute-start.3 = (bf16[432,1536]{1,0:T(8,128)(2,1)}, bf16[432,1536]{1,0:T(8,128)(2,1)}, u32[]{:S(2)}, u32[]{:S(2)}) collective-permute-start(bf16[432,1536]{1,0:T(8,128)(2,1)} %fusion.28), channel_id=1, source_target_pairs={{0,2},{2,0},{4,6},{6,4},{8,10},{10,8},{12,14},{14,12},{16,18},{18,... | collective-permute-start | bytes 3981320 | tf_op jit(solution)/shard_map/ppermute | solution.py:134
  24.9 10.7 %collective-permute-start.2 = (bf16[432,768]{1,0:T(8,128)(2,1)S(1)}, bf16[432,768]{1,0:T(8,128)(2,1)S(1)}, u32[]{:S(2)}, u32[]{:S(2)}) collective-permute-start(bf16[432,768]{1,0:T(8,128)(2,1)S(1)} %bitcast.36), channel_id=1, source_target_pairs={{0,1},{1,0},{2,3},{3,2},{4,5},{5,4},{6,7},{7,6},{8,9},{9,8},{10,11... | collective-permute-start | bytes 1990664 | tf_op jit(solution)/shard_map/ppermute | solution.py:145
  38.2 12.6 %collective-permute-start.4 = (bf16[432,1536]{1,0:T(8,128)(2,1)}, bf16[432,1536]{1,0:T(8,128)(2,1)}, u32[]{:S(2)}, u32[]{:S(2)}) collective-permute-start(bf16[432,1536]{1,0:T(8,128)(2,1)} %fusion.25), channel_id=1, source_target_pairs={{0,2},{2,0},{4,6},{6,4},{8,10},{10,8},{12,14},{14,12},{16,18},{18,... | collective-permute-start | bytes 3981320 | tf_op jit(solution)/shard_map/ppermute | solution.py:163
  68.4 29.4 %copy-start.14 = (bf16[1536,1536]{1,0:T(8,128)(2,1)}, bf16[1536,1536]{1,0:T(8,128)(2,1)S(1)}, u32[]{:S(2)}) copy-start(bf16[1536,1536]{1,0:T(8,128)(2,1)S(1)} %fusion.1) | copy-start | bytes 14155780
  68.5 18.4 %collective-permute-start.13 = (bf16[96,1536]{1,0:T(8,128)(2,1)S(1)}, bf16[96,1536]{1,0:T(8,128)(2,1)S(1)}, u32[]{:S(2)}, u32[]{:S(2)}) collective-permute-start(bf16[96,1536]{1,0:T(8,128)(2,1)S(1)} %get-tuple-element.176), channel_id=1, source_target_pairs={{0,4},{2,6},{8,0},{10,2},{16,8},{18,10},{24,16},{26,18},{28,24},{3... | collective-permute-start | bytes 884744 | tf_op jit(solution)/shard_map/ppermute | solution.py:95
  72.5 14.4 %collective-permute-start.10 = (bf16[96,1536]{1,0:T(8,128)(2,1)S(1)}, bf16[96,1536]{1,0:T(8,128)(2,1)S(1)}, u32[]{:S(2)}, u32[]{:S(2)}) collective-permute-start(bf16[96,1536]{1,0:T(8,128)(2,1)S(1)} %get-tuple-element.177), channel_id=1, source_target_pairs={{0,8},{2,10},{8,16},{10,18},{16,24},{18,26},{24,28},{26,30},{28,20... | collective-permute-start | bytes 884744 | tf_op jit(solution)/shard_map/ppermute | solution.py:95
  82.4 30.2 %copy-start.13 = (bf16[1536,1536]{1,0:T(8,128)(2,1)}, bf16[1536,1536]{1,0:T(8,128)(2,1)S(1)}, u32[]{:S(2)}) copy-start(bf16[1536,1536]{1,0:T(8,128)(2,1)S(1)} %fusion) | copy-start | bytes 14155780
  82.4 9.9 %collective-permute-start.19 = (bf16[96,1536]{1,0:T(8,128)(2,1)S(1)}, bf16[96,1536]{1,0:T(8,128)(2,1)S(1)}, u32[]{:S(2)}, u32[]{:S(2)}) collective-permute-start(bf16[96,1536]{1,0:T(8,128)(2,1)S(1)} %get-tuple-element.166), channel_id=1, source_target_pairs={{0,4},{2,6},{8,0},{10,2},{16,8},{18,10},{24,16},{26,18},{28,24},{3... | collective-permute-start | bytes 884744 | tf_op jit(solution)/shard_map/ppermute | solution.py:95
  82.5 9.9 %collective-permute-start.18 = (bf16[96,1536]{1,0:T(8,128)(2,1)S(1)}, bf16[96,1536]{1,0:T(8,128)(2,1)S(1)}, u32[]{:S(2)}, u32[]{:S(2)}) collective-permute-start(bf16[96,1536]{1,0:T(8,128)(2,1)S(1)} %get-tuple-element.167), channel_id=1, source_target_pairs={{0,8},{2,10},{8,16},{10,18},{16,24},{18,26},{24,28},{26,30},{28,20... | collective-permute-start | bytes 884744 | tf_op jit(solution)/shard_map/ppermute | solution.py:95
  86.8 12.1 %collective-permute-start.5 = (bf16[432,1536]{1,0:T(8,128)(2,1)S(1)}, bf16[432,1536]{1,0:T(8,128)(2,1)S(1)}, u32[]{:S(2)}, u32[]{:S(2)}) collective-permute-start(bf16[432,1536]{1,0:T(8,128)(2,1)S(1)} %fusion.22), channel_id=1, source_target_pairs={{0,2},{2,0},{4,6},{6,4},{8,10},{10,8},{12,14},{14,12},{16,18},{18,... | collective-permute-start | bytes 3981320 | tf_op jit(solution)/shard_map/ppermute | solution.py:180
  87.0 10.8 %collective-permute-start.14 = (bf16[96,1536]{1,0:T(8,128)(2,1)S(1)}, bf16[96,1536]{1,0:T(8,128)(2,1)S(1)}, u32[]{:S(2)}, u32[]{:S(2)}) collective-permute-start(bf16[96,1536]{1,0:T(8,128)(2,1)S(1)} %get-tuple-element.174), channel_id=1, source_target_pairs={{0,4},{2,6},{8,0},{10,2},{16,8},{18,10},{24,16},{26,18},{28,24},{3... | collective-permute-start | bytes 884744 | tf_op jit(solution)/shard_map/ppermute | solution.py:95
  87.2 10.7 %collective-permute-start.11 = (bf16[96,1536]{1,0:T(8,128)(2,1)S(1)}, bf16[96,1536]{1,0:T(8,128)(2,1)S(1)}, u32[]{:S(2)}, u32[]{:S(2)}) collective-permute-start(bf16[96,1536]{1,0:T(8,128)(2,1)S(1)} %get-tuple-element.175), channel_id=1, source_target_pairs={{0,8},{2,10},{8,16},{10,18},{16,24},{18,26},{24,28},{26,30},{28,20... | collective-permute-start | bytes 884744 | tf_op jit(solution)/shard_map/ppermute | solution.py:95
  101.7 4.3 %collective-permute-start.7 = (f32[2,432]{1,0:T(2,128)S(1)}, f32[2,432]{1,0:T(2,128)S(1)}, u32[]{:S(2)}, u32[]{:S(2)}) collective-permute-start(f32[2,432]{1,0:T(2,128)S(1)} %pad_maximum_fusion.7), channel_id=1, source_target_pairs={{0,1},{1,0},{2,3},{3,2},{4,5},{5,4},{6,7},{7,6},{8,9},{9,8},{10,11... | collective-permute-start | bytes 10376 | tf_op jit(solution)/shard_map/ppermute | solution.py:194
  103.2 16.0 %copy-start.12 = (bf16[3,144,768]{2,1,0:T(8,128)(2,1)S(1)}, bf16[3,144,768]{2,1,0:T(8,128)(2,1)}, u32[]{:S(2)}) copy-start(bf16[3,144,768]{2,1,0:T(8,128)(2,1)} %copy-done.11) | copy-start | bytes 1990660
  103.2 16.0 %copy-start.64 = (f32[768]{0:T(1024)S(1)}, f32[768]{0:T(1024)}, u32[]{:S(2)}) copy-start(f32[768]{0:T(1024)} %dynamic_slice.119) | copy-start | bytes 9220
  103.3 15.9 %collective-permute-start.6 = (bf16[432,768]{1,0:T(8,128)(2,1)S(1)}, bf16[432,768]{1,0:T(8,128)(2,1)S(1)}, u32[]{:S(2)}, u32[]{:S(2)}) collective-permute-start(bf16[432,768]{1,0:T(8,128)(2,1)S(1)} %dynamic-slice_convert_fusion), channel_id=1, source_target_pairs={{0,1},{1,0},{2,3},{3,2},{4,5},{5,4},{6,7},{7,6},{8,9},{9,8},{10,11... | collective-permute-start | bytes 1990664 | tf_op jit(solution)/shard_map/ppermute | solution.py:192
  103.9 7.6 %collective-permute-start.20 = (bf16[96,1536]{1,0:T(8,128)(2,1)S(1)}, bf16[96,1536]{1,0:T(8,128)(2,1)S(1)}, u32[]{:S(2)}, u32[]{:S(2)}) collective-permute-start(bf16[96,1536]{1,0:T(8,128)(2,1)S(1)} %get-tuple-element.26), channel_id=1, source_target_pairs={{0,8},{2,10},{8,16},{10,18},{16,24},{18,26},{24,28},{26,30},{28,20... | collective-permute-start | bytes 884744 | tf_op jit(solution)/shard_map/ppermute | solution.py:95
  105.6 7.0 %collective-permute-start.22 = (bf16[96,1536]{1,0:T(8,128)(2,1)S(1)}, bf16[96,1536]{1,0:T(8,128)(2,1)S(1)}, u32[]{:S(2)}, u32[]{:S(2)}) collective-permute-start(bf16[96,1536]{1,0:T(8,128)(2,1)S(1)} %get-tuple-element.27), channel_id=1, source_target_pairs={{0,4},{2,6},{8,0},{10,2},{16,8},{18,10},{24,16},{26,18},{28,24},{3... | collective-permute-start | bytes 884744 | tf_op jit(solution)/shard_map/ppermute | solution.py:95
  129.5 4.2 %collective-permute-start.26 = (bf16[7,7,768]{2,1,0:T(8,128)(2,1)S(1)}, bf16[7,7,768]{2,1,0:T(8,128)(2,1)S(1)}, u32[]{:S(2)}, u32[]{:S(2)}) collective-permute-start(bf16[7,7,768]{2,1,0:T(8,128)(2,1)S(1)} %multiply_convert_fusion.3), channel_id=1, source_target_pairs={{0,2},{2,0},{4,6},{6,4},{8,10},{10,8},{12,14},{14,12},{16,18},{18,... | collective-permute-start | bytes 225800 | tf_op jit(solution)/shard_map/ppermute | solution.py:238
  129.6 9.9 %collective-permute-start.23 = (bf16[96,1536]{1,0:T(8,128)(2,1)S(1)}, bf16[96,1536]{1,0:T(8,128)(2,1)S(1)}, u32[]{:S(2)}, u32[]{:S(2)}) collective-permute-start(bf16[96,1536]{1,0:T(8,128)(2,1)S(1)} %get-tuple-element.162), channel_id=1, source_target_pairs={{0,4},{2,6},{8,0},{10,2},{16,8},{18,10},{24,16},{26,18},{28,24},{3... | collective-permute-start | bytes 884744 | tf_op jit(solution)/shard_map/ppermute | solution.py:95
  130.2 10.1 %collective-permute-start.21 = (bf16[96,1536]{1,0:T(8,128)(2,1)S(1)}, bf16[96,1536]{1,0:T(8,128)(2,1)S(1)}, u32[]{:S(2)}, u32[]{:S(2)}) collective-permute-start(bf16[96,1536]{1,0:T(8,128)(2,1)S(1)} %get-tuple-element.163), channel_id=1, source_target_pairs={{0,8},{2,10},{8,16},{10,18},{16,24},{18,26},{24,28},{26,30},{28,20... | collective-permute-start | bytes 884744 | tf_op jit(solution)/shard_map/ppermute | solution.py:95
  131.7 16.8 %collective-permute-start.15 = (bf16[96,1536]{1,0:T(8,128)(2,1)S(1)}, bf16[96,1536]{1,0:T(8,128)(2,1)S(1)}, u32[]{:S(2)}, u32[]{:S(2)}) collective-permute-start(bf16[96,1536]{1,0:T(8,128)(2,1)S(1)} %copy-done.17), channel_id=1, source_target_pairs={{0,4},{2,6},{8,0},{10,2},{16,8},{18,10},{24,16},{26,18},{28,24},{3... | collective-permute-start | bytes 884744 | tf_op jit(solution)/shard_map/ppermute | solution.py:95
  132.5 16.1 %collective-permute-start.12 = (bf16[96,1536]{1,0:T(8,128)(2,1)S(1)}, bf16[96,1536]{1,0:T(8,128)(2,1)S(1)}, u32[]{:S(2)}, u32[]{:S(2)}) collective-permute-start(bf16[96,1536]{1,0:T(8,128)(2,1)S(1)} %copy-done.16), channel_id=1, source_target_pairs={{0,8},{2,10},{8,16},{10,18},{16,24},{18,26},{24,28},{26,30},{28,20... | collective-permute-start | bytes 884744 | tf_op jit(solution)/shard_map/ppermute | solution.py:95
  133.7 14.7 %collective-permute-start.29 = (bf16[7,7,768]{2,1,0:T(8,128)(2,1)S(1)}, bf16[7,7,768]{2,1,0:T(8,128)(2,1)S(1)}, u32[]{:S(2)}, u32[]{:S(2)}) collective-permute-start(bf16[7,7,768]{2,1,0:T(8,128)(2,1)S(1)} %add_convert_fusion.31), channel_id=1, source_target_pairs={{0,4},{2,6},{4,0},{6,2},{8,12},{10,14},{12,8},{14,10},{16,20},{18,... | collective-permute-start | bytes 225800 | tf_op jit(solution)/shard_map/ppermute | solution.py:238
  141.4 14.7 %collective-permute-start.24 = (bf16[96,1536]{1,0:T(8,128)(2,1)S(1)}, bf16[96,1536]{1,0:T(8,128)(2,1)S(1)}, u32[]{:S(2)}, u32[]{:S(2)}) collective-permute-start(bf16[96,1536]{1,0:T(8,128)(2,1)S(1)} %get-tuple-element.29), channel_id=1, source_target_pairs={{0,8},{2,10},{8,16},{10,18},{16,24},{18,26},{24,28},{26,30},{28,20... | collective-permute-start | bytes 884744 | tf_op jit(solution)/shard_map/ppermute | solution.py:95
  142.8 13.5 %collective-permute-start.25 = (bf16[96,1536]{1,0:T(8,128)(2,1)S(1)}, bf16[96,1536]{1,0:T(8,128)(2,1)S(1)}, u32[]{:S(2)}, u32[]{:S(2)}) collective-permute-start(bf16[96,1536]{1,0:T(8,128)(2,1)S(1)} %get-tuple-element.30), channel_id=1, source_target_pairs={{0,4},{2,6},{8,0},{10,2},{16,8},{18,10},{24,16},{26,18},{28,24},{3... | collective-permute-start | bytes 884744 | tf_op jit(solution)/shard_map/ppermute | solution.py:95
  148.4 5.7 %collective-permute-start.32 = (bf16[7,7,768]{2,1,0:T(8,128)(2,1)S(1)}, bf16[7,7,768]{2,1,0:T(8,128)(2,1)S(1)}, u32[]{:S(2)}, u32[]{:S(2)}) collective-permute-start(bf16[7,7,768]{2,1,0:T(8,128)(2,1)S(1)} %add_convert_fusion.30), channel_id=1, source_target_pairs={{0,8},{2,10},{4,12},{6,14},{8,0},{10,2},{12,4},{14,6},{16,24},{18,... | collective-permute-start | bytes 225800 | tf_op jit(solution)/shard_map/ppermute | solution.py:238
  149.7 39.3 %collective-permute-start.9 = (bf16[3,144,768]{2,1,0:T(8,128)(2,1)S(1)}, bf16[3,144,768]{2,1,0:T(8,128)(2,1)S(1)}, u32[]{:S(2)}, u32[]{:S(2)}) collective-permute-start(bf16[3,144,768]{2,1,0:T(8,128)(2,1)S(1)} %bitcast.33), channel_id=1, source_target_pairs={{2,0},{4,2},{6,4},{8,6},{10,8},{12,10},{14,12},{16,14},{18,16},{20... | collective-permute-start | bytes 1990664 | tf_op jit(solution)/shard_map/ppermute | solution.py:15
  151.0 39.2 %collective-permute-start.8 = (bf16[3,144,768]{2,1,0:T(8,128)(2,1)S(1)}, bf16[3,144,768]{2,1,0:T(8,128)(2,1)S(1)}, u32[]{:S(2)}, u32[]{:S(2)}) collective-permute-start(bf16[3,144,768]{2,1,0:T(8,128)(2,1)S(1)} %bitcast.34), channel_id=1, source_target_pairs={{0,2},{2,4},{4,6},{6,8},{8,10},{10,12},{12,14},{14,16},{16,18},{18... | collective-permute-start | bytes 1990664 | tf_op jit(solution)/shard_map/ppermute | solution.py:14
  154.1 14.1 %collective-permute-start.16 = (bf16[96,1536]{1,0:T(8,128)(2,1)S(1)}, bf16[96,1536]{1,0:T(8,128)(2,1)S(1)}, u32[]{:S(2)}, u32[]{:S(2)}) collective-permute-start(bf16[96,1536]{1,0:T(8,128)(2,1)S(1)} %get-tuple-element.24), channel_id=1, source_target_pairs={{0,8},{2,10},{8,16},{10,18},{16,24},{18,26},{24,28},{26,30},{28,20... | collective-permute-start | bytes 884744 | tf_op jit(solution)/shard_map/ppermute | solution.py:95
  156.2 12.6 %collective-permute-start.17 = (bf16[96,1536]{1,0:T(8,128)(2,1)S(1)}, bf16[96,1536]{1,0:T(8,128)(2,1)S(1)}, u32[]{:S(2)}, u32[]{:S(2)}) collective-permute-start(bf16[96,1536]{1,0:T(8,128)(2,1)S(1)} %get-tuple-element.25), channel_id=1, source_target_pairs={{0,4},{2,6},{8,0},{10,2},{16,8},{18,10},{24,16},{26,18},{28,24},{3... | collective-permute-start | bytes 884744 | tf_op jit(solution)/shard_map/ppermute | solution.py:95
  156.3 17.3 %collective-permute-start.43 = (bf16[7,7,768]{2,1,0:T(8,128)(2,1)S(1)}, bf16[7,7,768]{2,1,0:T(8,128)(2,1)S(1)}, u32[]{:S(2)}, u32[]{:S(2)}) collective-permute-start(bf16[7,7,768]{2,1,0:T(8,128)(2,1)S(1)} %add_convert_fusion.29), channel_id=1, source_target_pairs={{0,16},{2,18},{4,20},{6,22},{8,24},{10,26},{12,28},{14,30},{16,0},... | collective-permute-start | bytes 225800 | tf_op jit(solution)/shard_map/ppermute | solution.py:249
  168.2 6.7 %collective-permute-start.27 = (bf16[96,1536]{1,0:T(8,128)(2,1)S(1)}, bf16[96,1536]{1,0:T(8,128)(2,1)S(1)}, u32[]{:S(2)}, u32[]{:S(2)}) collective-permute-start(bf16[96,1536]{1,0:T(8,128)(2,1)S(1)} %get-tuple-element.32), channel_id=1, source_target_pairs={{0,8},{2,10},{8,16},{10,18},{16,24},{18,26},{24,28},{26,30},{28,20... | collective-permute-start | bytes 884744 | tf_op jit(solution)/shard_map/ppermute | solution.py:95
  168.8 9.1 %collective-permute-start.28 = (bf16[96,1536]{1,0:T(8,128)(2,1)S(1)}, bf16[96,1536]{1,0:T(8,128)(2,1)S(1)}, u32[]{:S(2)}, u32[]{:S(2)}) collective-permute-start(bf16[96,1536]{1,0:T(8,128)(2,1)S(1)} %get-tuple-element.33), channel_id=1, source_target_pairs={{0,4},{2,6},{8,0},{10,2},{16,8},{18,10},{24,16},{26,18},{28,24},{3... | collective-permute-start | bytes 884744 | tf_op jit(solution)/shard_map/ppermute | solution.py:95
  173.6 10.4 %collective-permute-start.39 = (bf16[96,1536]{1,0:T(8,128)(2,1)S(1)}, bf16[96,1536]{1,0:T(8,128)(2,1)S(1)}, u32[]{:S(2)}, u32[]{:S(2)}) collective-permute-start(bf16[96,1536]{1,0:T(8,128)(2,1)S(1)} %get-tuple-element.168), channel_id=1, source_target_pairs={{0,4},{2,6},{8,0},{10,2},{16,8},{18,10},{24,16},{26,18},{28,24},{3... | collective-permute-start | bytes 884744 | tf_op jit(solution)/shard_map/ppermute | solution.py:95
  174.9 9.0 %collective-permute-start.36 = (bf16[96,1536]{1,0:T(8,128)(2,1)S(1)}, bf16[96,1536]{1,0:T(8,128)(2,1)S(1)}, u32[]{:S(2)}, u32[]{:S(2)}) collective-permute-start(bf16[96,1536]{1,0:T(8,128)(2,1)S(1)} %get-tuple-element.169), channel_id=1, source_target_pairs={{0,8},{2,10},{8,16},{10,18},{16,24},{18,26},{24,28},{26,30},{28,20... | collective-permute-start | bytes 884744 | tf_op jit(solution)/shard_map/ppermute | solution.py:95
  179.1 12.2 %collective-permute-start.30 = (bf16[96,1536]{1,0:T(8,128)(2,1)S(1)}, bf16[96,1536]{1,0:T(8,128)(2,1)S(1)}, u32[]{:S(2)}, u32[]{:S(2)}) collective-permute-start(bf16[96,1536]{1,0:T(8,128)(2,1)S(1)} %get-tuple-element.34), channel_id=1, source_target_pairs={{0,8},{2,10},{8,16},{10,18},{16,24},{18,26},{24,28},{26,30},{28,20... | collective-permute-start | bytes 884744 | tf_op jit(solution)/shard_map/ppermute | solution.py:95
  183.9 10.8 %collective-permute-start.31 = (bf16[96,1536]{1,0:T(8,128)(2,1)S(1)}, bf16[96,1536]{1,0:T(8,128)(2,1)S(1)}, u32[]{:S(2)}, u32[]{:S(2)}) collective-permute-start(bf16[96,1536]{1,0:T(8,128)(2,1)S(1)} %get-tuple-element.35), channel_id=1, source_target_pairs={{0,4},{2,6},{8,0},{10,2},{16,8},{18,10},{24,16},{26,18},{28,24},{3... | collective-permute-start | bytes 884744 | tf_op jit(solution)/shard_map/ppermute | solution.py:95
  185.2 15.9 %collective-permute-start.40 = (bf16[96,1536]{1,0:T(8,128)(2,1)S(1)}, bf16[96,1536]{1,0:T(8,128)(2,1)S(1)}, u32[]{:S(2)}, u32[]{:S(2)}) collective-permute-start(bf16[96,1536]{1,0:T(8,128)(2,1)S(1)} %get-tuple-element.152), channel_id=1, source_target_pairs={{0,4},{2,6},{8,0},{10,2},{16,8},{18,10},{24,16},{26,18},{28,24},{3... | collective-permute-start | bytes 884744 | tf_op jit(solution)/shard_map/ppermute | solution.py:95
  189.0 13.1 %collective-permute-start.37 = (bf16[96,1536]{1,0:T(8,128)(2,1)S(1)}, bf16[96,1536]{1,0:T(8,128)(2,1)S(1)}, u32[]{:S(2)}, u32[]{:S(2)}) collective-permute-start(bf16[96,1536]{1,0:T(8,128)(2,1)S(1)} %get-tuple-element.153), channel_id=1, source_target_pairs={{0,8},{2,10},{8,16},{10,18},{16,24},{18,26},{24,28},{26,30},{28,20... | collective-permute-start | bytes 884744 | tf_op jit(solution)/shard_map/ppermute | solution.py:95
  203.6 15.4 %collective-permute-start.41 = (bf16[96,1536]{1,0:T(8,128)(2,1)S(1)}, bf16[96,1536]{1,0:T(8,128)(2,1)S(1)}, u32[]{:S(2)}, u32[]{:S(2)}) collective-permute-start(bf16[96,1536]{1,0:T(8,128)(2,1)S(1)} %get-tuple-element.150), channel_id=1, source_target_pairs={{0,4},{2,6},{8,0},{10,2},{16,8},{18,10},{24,16},{26,18},{28,24},{3... | collective-permute-start | bytes 884744 | tf_op jit(solution)/shard_map/ppermute | solution.py:95
  205.7 13.3 %collective-permute-start.38 = (bf16[96,1536]{1,0:T(8,128)(2,1)S(1)}, bf16[96,1536]{1,0:T(8,128)(2,1)S(1)}, u32[]{:S(2)}, u32[]{:S(2)}) collective-permute-start(bf16[96,1536]{1,0:T(8,128)(2,1)S(1)} %get-tuple-element.151), channel_id=1, source_target_pairs={{0,8},{2,10},{8,16},{10,18},{16,24},{18,26},{24,28},{26,30},{28,20... | collective-permute-start | bytes 884744 | tf_op jit(solution)/shard_map/ppermute | solution.py:95
  216.9 8.8 %collective-permute-start.33 = (bf16[96,1536]{1,0:T(8,128)(2,1)S(1)}, bf16[96,1536]{1,0:T(8,128)(2,1)S(1)}, u32[]{:S(2)}, u32[]{:S(2)}) collective-permute-start(bf16[96,1536]{1,0:T(8,128)(2,1)S(1)} %get-tuple-element.38), channel_id=1, source_target_pairs={{0,8},{2,10},{8,16},{10,18},{16,24},{18,26},{24,28},{26,30},{28,20... | collective-permute-start | bytes 884744 | tf_op jit(solution)/shard_map/ppermute | solution.py:95
  218.9 10.1 %collective-permute-start.34 = (bf16[96,1536]{1,0:T(8,128)(2,1)S(1)}, bf16[96,1536]{1,0:T(8,128)(2,1)S(1)}, u32[]{:S(2)}, u32[]{:S(2)}) collective-permute-start(bf16[96,1536]{1,0:T(8,128)(2,1)S(1)} %get-tuple-element.39), channel_id=1, source_target_pairs={{0,4},{2,6},{8,0},{10,2},{16,8},{18,10},{24,16},{26,18},{28,24},{3... | collective-permute-start | bytes 884744 | tf_op jit(solution)/shard_map/ppermute | solution.py:95
  220.3 10.0 %collective-permute-start.42 = (bf16[96,1536]{1,0:T(8,128)(2,1)S(1)}, bf16[96,1536]{1,0:T(8,128)(2,1)S(1)}, u32[]{:S(2)}, u32[]{:S(2)}) collective-permute-start(bf16[96,1536]{1,0:T(8,128)(2,1)S(1)} %get-tuple-element.144), channel_id=1, source_target_pairs={{0,2},{2,0},{4,6},{6,4},{8,10},{10,8},{12,14},{14,12},{16,18},{18,... | collective-permute-start | bytes 884744 | tf_op jit(solution)/shard_map/ppermute | solution.py:105
  230.1 1.6 collective-permute-start.35
  (67 other events, 536.1 us)
